TPU v7x, 256 devices: a whole 4x4x8 slice. The times are simulated.
256 devices in a mesh: batch: 32 (over y, x, core), tensor: 8 (over z).
Axes of the slice: x: 4, y: 4, z: 8, core: 2. Of those that a mesh axis runs over, the one named last changes fastest.
Arguments:
- normed_hidden_rows: bfloat16 [4, 512, 8192], P(None, 'batch', 'tensor'), may hold values from -6 to 6
- queries: bfloat16 [4, 512, 8192], P(None, 'batch', 'tensor'), may hold values from -6 to 6
- key_weight: bfloat16 [8192, 1024], P('tensor'), may hold values from -0.0625 to 0.0625
- value_weight: bfloat16 [8192, 1024], P('tensor'), may hold values from -0.0625 to 0.0625
- adapter_down: bfloat16 [1024, 64, 8192], P('batch', None, 'tensor'), may hold values from -0.0625 to 0.0625
- adapter_up: bfloat16 [1024, 64, 1024], P('batch', None, 'tensor'), may hold values from -0.75 to 0.75
- adapter_ids: int32 [512], P('batch'), may hold values from 0 to 1023, as said below
- owner_map: int32 [1024], replicated, may hold values from 0 to 1023, as said below
- cache_keys: bfloat16 [512, 8, 256, 128], P('batch', 'tensor'), may hold values from -6 to 6
- cache_values: bfloat16 [512, 8, 256, 128], P('batch', 'tensor'), may hold values from -6 to 6
- cache_lengths: int32 [512], P('batch'), may hold values from 2 to 256, as said below
Outputs:
- new_keys: bfloat16 [4, 512, 1024], P(None, 'batch', 'tensor')
- incoming_values: bfloat16 [4, 512, 1024], P(None, 'batch', 'tensor')
- attention: bfloat16 [4, 512, 8192], P(None, 'batch', 'tensor')
Inputs may be any that keep to these rules, and one draw needn't show every extreme that they name: A permutation: adapter a is stored in row owner_map[a] of adapter_down and adapter_up, whose owner is owner_map[a] // 32. `adapter_ids`: among the 16 requests of one device at most 2 have adapters of one owner; in every draw one owner has exactly 2 requests from every device. `cache_lengths`: some request has exactly 256.
All inputs are finite; a program needn't handle non-finite values.
Results may differ from a plain program's by a relative error of at most 0.0095.
Values may be sent and summed in bfloat16 or wider, within the bound.
No kernel may reach another device: no remote copies, remote signals or barrier semaphores. Data moves between devices by JAX's collectives and lax.ppermute only.
A program may use at most 128 MiB of HBM per device.

v0:
```python
import math

import jax
import jax.numpy as jnp
from jax import lax
from jax.sharding import PartitionSpec as P

HEADS = 64
KV_HEADS = 8
CAP = 2


ADAPTER_SCALE = 0.5
MASKED = -1e30


def storage_rows(adapter_ids, owner_map):
    every_slot = jnp.arange(owner_map.shape[0], dtype=jnp.int32)
    matches = adapter_ids[:, None] == every_slot[None, :]
    return jnp.sum(jnp.where(matches, owner_map[None, :], 0), axis=1)


def slot_tables(adapter_slot_rows, per_owner, owners):
    owner_index = adapter_slot_rows // per_owner
    local_row = adapter_slot_rows % per_owner
    request_order = jnp.arange(adapter_slot_rows.shape[0], dtype=jnp.int32)
    same_owner = (owner_index[:, None] == owner_index[None, :]) & (
        request_order[None, :] < request_order[:, None]
    )
    slot_rank = jnp.sum(same_owner.astype(jnp.int32), axis=1)
    owner_range = jnp.arange(owners, dtype=jnp.int32)
    rank_range = jnp.arange(CAP, dtype=jnp.int32)
    placement = (owner_index[:, None, None] == owner_range[None, :, None]) & (
        slot_rank[:, None, None] == rank_range[None, None, :]
    )
    wanted = jnp.sum(jnp.where(placement, local_row[:, None, None], 0), axis=0)
    source = jnp.sum(jnp.where(placement, request_order[:, None, None], 0), axis=0)
    position = owner_index * CAP + slot_rank
    return (wanted, source, position)


def per_device(
    normed_hidden_rows,
    queries,
    key_weight,
    value_weight,
    adapter_down,
    adapter_up,
    adapter_ids,
    owner_map,
    cache_keys,
    cache_values,
    cache_lengths,
):
    step_count, requests, feature_cols = normed_hidden_rows.shape
    owners = lax.axis_size("batch")
    tensor_size = lax.axis_size("tensor")
    per_owner = adapter_down.shape[0]
    local_heads = cache_keys.shape[1]
    head_dim = cache_keys.shape[3]
    all_heads = local_heads * tensor_size
    group_size = HEADS // KV_HEADS
    tokens = normed_hidden_rows.reshape(step_count * requests, feature_cols)
    key_heads = key_weight.reshape(feature_cols, all_heads, head_dim)
    value_heads = value_weight.reshape(feature_cols, all_heads, head_dim)
    key_term = jnp.einsum("md,dhe->hme", tokens, key_heads, preferred_element_type=jnp.float32)
    value_term = jnp.einsum("md,dhe->hme", tokens, value_heads, preferred_element_type=jnp.float32)
    summed = lax.psum_scatter(
        jnp.concatenate([key_term, value_term], axis=2), "tensor", scatter_dimension=0, tiled=True
    )
    summed = jnp.transpose(summed, (1, 0, 2)).reshape(
        step_count, requests, local_heads, 2 * head_dim
    )
    base_keys = summed[..., :head_dim].reshape(step_count, requests, local_heads * head_dim)
    frozen_value_rows = summed[..., head_dim:].reshape(step_count, requests, local_heads * head_dim)
    adapter_slot_rows = storage_rows(adapter_ids, owner_map)
    wanted, source, position = slot_tables(adapter_slot_rows, per_owner, owners)
    granted = lax.all_to_all(wanted, "batch", split_axis=0, concat_axis=0, tiled=True)
    down_blocks = jnp.take(adapter_down, granted.reshape(-1), axis=0)
    up_blocks = jnp.take(adapter_up, granted.reshape(-1), axis=0)
    fetched_down, fetched_up = (
        lax.all_to_all(down_blocks, "batch", split_axis=0, concat_axis=0, tiled=True),
        lax.all_to_all(up_blocks, "batch", split_axis=0, concat_axis=0, tiled=True),
    )
    request_down = jnp.take(fetched_down, position, axis=0)
    request_up = jnp.take(fetched_up, position, axis=0)
    partial_sum = jnp.einsum(
        "smd,mrd->smr", normed_hidden_rows, request_down, preferred_element_type=jnp.float32
    )
    shrink = lax.psum(partial_sum, "tensor")
    adapter_correction = jnp.einsum(
        "smr,mre->sme", shrink.astype(jnp.bfloat16), request_up, preferred_element_type=jnp.float32
    )
    new_keys = base_keys.astype(jnp.bfloat16)
    incoming_values = (frozen_value_rows + ADAPTER_SCALE * adapter_correction).astype(jnp.bfloat16)
    score_scale = 1.0 / math.sqrt(head_dim)
    query_heads = queries.reshape(step_count, requests, local_heads, group_size, head_dim)
    fresh_keys = new_keys.reshape(step_count, requests, local_heads, head_dim)
    fresh_values = incoming_values.reshape(step_count, requests, local_heads, head_dim)
    cached = (
        jnp.einsum("srkgd,rkcd->srkgc", query_heads, cache_keys, preferred_element_type=jnp.float32)
        * score_scale
    )
    recent = (
        jnp.einsum("srkgd,trkd->srkgt", query_heads, fresh_keys, preferred_element_type=jnp.float32)
        * score_scale
    )
    visible = jnp.arange(cache_keys.shape[2], dtype=jnp.int32)[None, :] < cache_lengths[:, None]
    cached = jnp.where(visible[None, :, None, None, :], cached, MASKED)
    step_index = jnp.arange(step_count, dtype=jnp.int32)
    causal = step_index[None, :] <= step_index[:, None]
    recent = jnp.where(causal[:, None, None, None, :], recent, MASKED)
    highest = jnp.maximum(jnp.max(cached, axis=-1), jnp.max(recent, axis=-1))[..., None]
    cached_exp = jnp.exp(cached - highest)
    recent_exp = jnp.exp(recent - highest)
    total = jnp.sum(cached_exp, axis=-1, keepdims=True) + jnp.sum(
        recent_exp, axis=-1, keepdims=True
    )
    cached_weights = (cached_exp / total).astype(jnp.bfloat16)
    recent_weights = (recent_exp / total).astype(jnp.bfloat16)
    mixed = jnp.einsum(
        "srkgc,rkcd->srkgd", cached_weights, cache_values, preferred_element_type=jnp.float32
    )
    mixed = mixed + jnp.einsum(
        "srkgt,trkd->srkgd", recent_weights, fresh_values, preferred_element_type=jnp.float32
    )
    attention = mixed.reshape(step_count, requests, local_heads * group_size * head_dim).astype(
        jnp.bfloat16
    )
    return (new_keys, incoming_values, attention)


def solution(mesh):
    placed = (
        P(None, "batch", "tensor"),
        P(None, "batch", "tensor"),
        P("tensor", None),
        P("tensor", None),
        P("batch", None, "tensor"),
        P("batch", None, "tensor"),
        P("batch"),
        P(),
        P("batch", "tensor", None, None),
        P("batch", "tensor", None, None),
        P("batch"),
    )
    return jax.shard_map(
        per_device,
        mesh=mesh,
        in_specs=placed,
        out_specs=(
            P(None, "batch", "tensor"),
            P(None, "batch", "tensor"),
            P(None, "batch", "tensor"),
        ),
        check_vma=False,
    )
```

profile of v0, /device:TPU:0, one launch (start us, length us, event | category | flops | bytes accessed | tf_op | source)
XLA Modules:
  0.0 215.8 jit_solution(18298163647144003577)
XLA Ops:
  7.2 1.0 select_reduce_fusion
  8.7 12.7 %all_to_all.19 = s32[32,1,2]{2,1,0:T(1,128)S(1)} all-to-all(s32[32,1,2]{2,1,0:T(1,128)S(1)} %copy.51), channel_id=1, replica_groups=mesh['batch'=32,'tensor'=8] {'batch'}, dimensions={0} | all-to-all | bytes 512 | tf_op jit(solution)/shard_map/all_to_all | solution.py:78
  21.5 0.5 broadcast.342
  22.0 0.7 reduce.9
  22.9 7.5 %gather_fusion.2 = bf16[64,64,1024]{2,1,0:T(8,128)(2,1)} fusion(bf16[32,64,1024]{2,1,0:T(8,128)(2,1)} %param.15, s32[1024]{0:T(1024)S(1)} %pad_clamp_fusion.1), kind=kCustom, calls=%fused_computation.2 | custom fusion | bytes 16777472 | tf_op jit(solution)/shard_map/jit(_take)/gather | solution.py:79
  30.4 1.8 gather_fusion
  32.2 1.2 broadcast_select_fusion.1
  33.3 3.9 %all-to-all-start.1 = ((bf16[64,64,128]{2,1,0:T(8,128)(2,1)}), bf16[64,64,128]{2,1,0:T(8,128)(2,1)S(1)}, u32[]{:S(2)}, u32[]{:S(2)}) async-start(bf16[64,64,128]{2,1,0:T(8,128)(2,1)} %broadcast_select_fusion.1), calls=%async_computation.2 | async-start | bytes 2097152 | tf_op jit(solution)/shard_map/all_to_all | solution.py:83
  37.3 7.5 %broadcast_select_fusion = bf16[64,64,1024]{2,1,0:T(8,128)(2,1)} fusion(bf16[64,64,1024]{2,1,0:T(8,128)(2,1)} %gather_fusion.2, pred[64]{0:T(512)(128)(4,1)S(1)} %compare_and_fusion), kind=kLoop, calls=%fused_computation.4 | loop fusion | flops 4194304 | bytes 16777280 | tf_op jit(solution)/shard_map/jit(_take)/select_n | solution.py:79
  44.8 9.9 %all-to-all-done.1 = bf16[64,64,128]{2,1,0:T(8,128)(2,1)S(1)} async-done(((bf16[64,64,128]{2,1,0:T(8,128)(2,1)}), bf16[64,64,128]{2,1,0:T(8,128)(2,1)S(1)}, u32[]{:S(2)}, u32[]{:S(2)}) %all-to-all-start.1) | async-done | bytes 1048608 | tf_op jit(solution)/shard_map/all_to_all | solution.py:83
  54.6 1.0 copy-done.1
  55.6 5.0 %all-to-all-start.2 = ((bf16[64,64,1024]{2,1,0:T(8,128)(2,1)}), bf16[64,64,1024]{2,1,0:T(8,128)(2,1)}, u32[]{:S(2)}, u32[]{:S(2)}) async-start(bf16[64,64,1024]{2,1,0:T(8,128)(2,1)} %broadcast_select_fusion), calls=%async_computation.3 | async-start | bytes 16777216 | tf_op jit(solution)/shard_map/all_to_all | solution.py:82
  60.7 0.5 fusion.12
  61.2 1.1 copy-done.4
  62.2 0.5 fusion.15
  62.7 0.9 pad_maximum_fusion
  63.8 1.8 fusion.52
  65.5 1.8 gather_fusion.1
  67.4 36.8 %reduce-scatter.2.cloned.1.call-done = f32[1,64,256]{2,1,0:T(8,128)} async-done(((f32[8,64,256]{2,1,0:T(8,128)}), f32[1,64,256]{2,1,0:T(8,128)}) %reduce-scatter.2.cloned.1.call-update) | async-done | bytes 65552 | tf_op jit(solution)/shard_map/reduce_scatter | solution.py:68
  104.2 0.8 slice.17
  104.9 0.8 slice.19
  105.7 0.6 copy.55
  106.3 0.7 fusion.53
  107.2 0.3 fusion.31
  107.5 2.3 %convolution_bitcast_fusion = f32[16,128,4,8]{1,3,2,0:T(8,128)} fusion(bf16[16,1,256,128]{3,2,1,0:T(8,128)(2,1)} %param.20, f32[4,16,1,8,256]{4,3,0,1,2:T(8,128)S(1)} %get-tuple-element.18, f32[4,16,8]{2,0,1:T(4,128)S(1)} %add.117, f32[4,16,8]{2,0,1:T(4,128)S(1)} %max.9), kind=kOutput, calls=%fused_computation.21 | convolution fusion | flops 33947648 | bytes 1839104 | tf_op jit(solution)/shard_map/srkgc,rkcd->srkgd/dot_general | solution.py:121
  109.7 56.7 %all-to-all-done.2 = bf16[64,64,1024]{2,1,0:T(8,128)(2,1)} async-done(((bf16[64,64,1024]{2,1,0:T(8,128)(2,1)}), bf16[64,64,1024]{2,1,0:T(8,128)(2,1)}, u32[]{:S(2)}, u32[]{:S(2)}) %all-to-all-start.2) | async-done | bytes 8388640 | tf_op jit(solution)/shard_map/all_to_all | solution.py:82
  166.5 5.5 %gather_fusion.3 = bf16[16,64,1024]{2,1,0:T(8,128)(2,1)} fusion(bf16[64,64,1024]{2,1,0:T(8,128)(2,1)} %all-to-all-done.2, s32[1024]{0:T(1024)S(1)} %pad_clamp_fusion), kind=kCustom, calls=%fused_computation.3 | custom fusion | bytes 4194368 | tf_op jit(solution)/shard_map/jit(_take)/gather | solution.py:85
  171.9 2.4 %fusion.21 = f32[4,16,64]{2,0,1:T(4,128)S(1)} fusion(bf16[16,64,1024]{2,1,0:T(8,128)(2,1)} %gather_fusion.3, pred[16]{0:T(512)(128)(4,1)S(1)} %compare_and_fusion.1, bf16[4,16,1024]{2,1,0:T(8,128)(2,1)S(1)} %copy-done.5), kind=kOutput, calls=%fused_computation.26 | convolution fusion | flops 9437184 | bytes 2244624 | tf_op jit(solution)/shard_map/smd,mrd->smr/dot_general | solution.py:87
  174.3 32.8 %psum.7 = bf16[4,16,64]{2,0,1:T(4,128)(2,1)S(1)} all-reduce(f32[4,16,64]{2,0,1:T(4,128)S(1)} %fusion.21), channel_id=1, replica_groups=mesh['batch'=32,'tensor'=8] {'tensor'}, use_global_device_ids=true, to_apply=%region_4.5 | all-reduce | flops 4096 | bytes 24576 | tf_op jit(solution)/shard_map/psum | solution.py:90
  207.3 0.6 copy.56
  207.9 0.3 fusion.19
  208.2 0.7 copy.57
  (37 shorter events, 1.4 us)
Async XLA Ops:
  7.2 53.5 %copy-start = (bf16[1024,1024]{1,0:T(8,128)(2,1)S(1)}, bf16[1024,1024]{1,0:T(8,128)(2,1)}, u32[]{:S(2)}) copy-start(bf16[1024,1024]{1,0:T(8,128)(2,1)} %param.13) | copy-start | bytes 6291460
  33.3 21.3 %all-to-all-start.1 = ((bf16[64,64,128]{2,1,0:T(8,128)(2,1)}), bf16[64,64,128]{2,1,0:T(8,128)(2,1)S(1)}, u32[]{:S(2)}, u32[]{:S(2)}) async-start(bf16[64,64,128]{2,1,0:T(8,128)(2,1)} %broadcast_select_fusion.1), calls=%async_computation.2 | async-start | bytes 2097152 | tf_op jit(solution)/shard_map/all_to_all | solution.py:83
  44.7 15.9 %copy-start.5 = (bf16[4,16,1024]{2,1,0:T(8,128)(2,1)S(1)}, bf16[4,16,1024]{2,1,0:T(8,128)(2,1)}, u32[]{:S(2)}) copy-start(bf16[4,16,1024]{2,1,0:T(8,128)(2,1)} %param.11) | copy-start | bytes 393220
  54.6 1.0 copy-start.1
  55.6 110.8 %all-to-all-start.2 = ((bf16[64,64,1024]{2,1,0:T(8,128)(2,1)}), bf16[64,64,1024]{2,1,0:T(8,128)(2,1)}, u32[]{:S(2)}, u32[]{:S(2)}) async-start(bf16[64,64,1024]{2,1,0:T(8,128)(2,1)} %broadcast_select_fusion), calls=%async_computation.3 | async-start | bytes 16777216 | tf_op jit(solution)/shard_map/all_to_all | solution.py:82
  60.6 43.6 %reduce-scatter.2.cloned.1.call-start = ((), (), s32[]{:S(2)}) async-start(), calls=%async_computation.4 | async-start | bytes 589824 | tf_op jit(solution)/shard_map/reduce_scatter | solution.py:68
  60.6 1.6 copy-start.4
  62.2 1.4 copy-start.2
  62.2 1.5 copy-start.3
  171.9 36.0 %copy-start.6 = (f32[16,128,4,8]{1,3,2,0:T(8,128)S(1)}, f32[16,128,4,8]{1,3,2,0:T(8,128)}, u32[]{:S(2)}) copy-start(f32[16,128,4,8]{1,3,2,0:T(8,128)} %convolution_bitcast_fusion) | copy-start | bytes 786436
Sparse Core Ops, SparseCore 0:
  63.9 40.1 reduce-scatter.1
where the time goes:
time: 217 us; the launch traced here: 216 us
  waiting for transfers between devices  103 us (47%)
  blocking collectives  45.5 us (21%)
  local copies, waits for them, and re-layouts  23 us (11%)
  between operations  14.3 us (7%)
  other arithmetic  12.1 us (6%)
  starting transfers between devices  8.93 us (4%)
  matrix products  8.55 us (4%)
    all_to_all x1, waiting for transfers between devices, per_device(): lax.all_to_all(down_blocks, 'batch', split_axis=0, concat_axis=0, tiled=T...  56.7 us
    reduce_scatter x1, waiting for transfers between devices, per_device(): lax.psum_scatter(jnp.concatenate([key_term, value_term], axis=2), 'tensor...  36.8 us
    psum x1, blocking collectives, per_device(): shrink = lax.psum(partial_sum, 'tensor')  32.8 us
    all_to_all x1, blocking collectives, per_device(): lax.all_to_all(wanted, 'batch', split_axis=0, concat_axis=0, tiled=True)  12.7 us
    all_to_all x1, waiting for transfers between devices, per_device(): lax.all_to_all(up_blocks, 'batch', split_axis=0, concat_axis=0, tiled=True)  9.87 us
    gather x1, local copies, waits for them, and re-layouts, per_device(): down_blocks = jnp.take(adapter_down, granted.reshape(-1), axis=0)  7.54 us
    select_n x1, other arithmetic, per_device(): down_blocks = jnp.take(adapter_down, granted.reshape(-1), axis=0)  7.46 us
    gather x1, local copies, waits for them, and re-layouts, per_device(): request_down = jnp.take(fetched_down, position, axis=0)  5.45 us
  transfers between devices with their start and end apart: 3, of which 3 were waited for; matrix products, arithmetic and copies ran while one was open for 9% of the time, Pallas kernels for 0%

commit v1 on v0

v1 whole, which is shorter than its diff:
```python
import math

import jax
import jax.numpy as jnp
from jax import lax
from jax.experimental import pallas as pl
from jax.experimental.pallas import tpu as pltpu
from jax.sharding import PartitionSpec as P

HEADS = 64
KV_HEADS = 8
CAP = 2

ADAPTER_SCALE = 0.5
MASKED = -1e30

F32 = jnp.float32
BF16 = jnp.bfloat16
LANES = 128
VMEM = pl.BlockSpec(memory_space=pltpu.VMEM)
SMEM = pl.BlockSpec(memory_space=pltpu.SMEM)


def params(*semantics):
    return pltpu.CompilerParams(
        dimension_semantics=semantics or None, vmem_limit_bytes=16 * 1024 * 1024
    )


def iota(shape, dim):
    return lax.broadcasted_iota(jnp.int32, shape, dim)


def contract_last(a, b):
    return lax.dot_general(a, b, (((1,), (1,)), ((), ())), preferred_element_type=F32)


def pack_kernel(ids, owner_map, x, packed, slot_of_token, counts, *, per_owner, owners):
    steps, requests, cols = x.shape
    tokens = steps * requests
    slot_rows = packed.shape[0]
    for o in range(owners):
        counts[o] = 0
    token = iota((tokens, LANES), 0) % requests
    column = iota((1, tokens), 1) % requests
    slot_sub = jnp.zeros((tokens, LANES), jnp.int32)
    row_sub = jnp.zeros((tokens, LANES), jnp.int32)
    slot_lane = jnp.zeros((1, tokens), jnp.int32)
    for r in range(requests):
        storage = owner_map[ids[r]]
        owner = storage // per_owner
        rank = counts[owner]
        counts[owner] = rank + 1
        slot = owner * CAP + rank
        slot_sub = jnp.where(token == r, slot, slot_sub)
        row_sub = jnp.where(token == r, storage - owner * per_owner, row_sub)
        slot_lane = jnp.where(column == r, slot, slot_lane)
    slot_of_token[...] = slot_sub
    place = iota((slot_rows, tokens), 0)
    source = iota((slot_rows, tokens), 1)
    chosen = (place // steps == slot_lane) & (place % steps == source // requests)
    chosen = jnp.where(chosen, 1.0, 0.0).astype(BF16)
    rows = x[...].reshape(tokens, cols)
    packed[:, :cols] = jnp.dot(chosen, rows, preferred_element_type=F32).astype(BF16)
    packed[:, cols:] = jnp.dot(
        chosen, row_sub.astype(F32).astype(BF16), preferred_element_type=F32
    ).astype(BF16)


def pack(adapter_ids, owner_map, x, per_owner, owners):
    steps, requests, cols = x.shape
    slot_rows = owners * CAP * steps
    kernel = lambda *refs: pack_kernel(*refs, per_owner=per_owner, owners=owners)
    return pl.pallas_call(
        kernel,
        out_shape=(
            jax.ShapeDtypeStruct((slot_rows, cols + LANES), BF16),
            jax.ShapeDtypeStruct((steps * requests, LANES), jnp.int32),
        ),
        in_specs=[SMEM, SMEM, VMEM],
        out_specs=(VMEM, VMEM),
        scratch_shapes=[pltpu.SMEM((owners,), jnp.int32)],
        compiler_params=params(),
        name="pack",
    )(adapter_ids, owner_map, x)


def project_kernel(x, key_weight, value_weight, out):
    tokens = out.shape[1] // 2
    rows = x[...].reshape(tokens, x.shape[2])
    out[0, :tokens] = jnp.dot(rows, key_weight[...], preferred_element_type=F32).astype(BF16)
    out[0, tokens:] = jnp.dot(rows, value_weight[...], preferred_element_type=F32).astype(BF16)


def project(x, key_weight, value_weight, heads):
    steps, requests, cols = x.shape
    head_dim = key_weight.shape[1] // heads
    tokens = steps * requests
    weight = pl.BlockSpec((cols, head_dim), lambda h: (0, h))
    return pl.pallas_call(
        project_kernel,
        grid=(heads,),
        out_shape=jax.ShapeDtypeStruct((heads, 2 * tokens, head_dim), BF16),
        in_specs=[pl.BlockSpec(x.shape, lambda h: (0, 0, 0)), weight, weight],
        out_specs=pl.BlockSpec((1, 2 * tokens, head_dim), lambda h: (h, 0, 0)),
        compiler_params=params("arbitrary"),
        cost_estimate=pl.CostEstimate(
            flops=4 * tokens * cols * heads * head_dim,
            bytes_accessed=4 * cols * heads * head_dim,
            transcendentals=0,
        ),
        name="project",
    )(x, key_weight, value_weight)


def cached_kernel(lengths, q, keys, values, out, highest, total, q_rows, *, scale):
    steps, requests, cols = q.shape
    positions, head_dim = keys.shape[2], keys.shape[3]
    groups = cols // head_dim
    rows = steps * groups
    per_step = keys.shape[0]
    block = pl.program_id(0)

    @pl.when(block == 0)
    def _():
        for s in range(steps):
            for g in range(groups):
                start = (s * groups + g) * requests
                q_rows[start : start + requests] = q[
                    s, :, g * head_dim : (g + 1) * head_dim
                ].astype(F32)

    position = iota((rows, positions), 1)
    for i in range(per_step):
        r = block * per_step + i
        mine = pl.ds(r, rows, stride=requests)
        scores = contract_last(q_rows[mine, :].astype(BF16), keys[i, 0]) * scale
        scores = jnp.where(position < lengths[r], scores, MASKED)
        top = jnp.max(scores, axis=1, keepdims=True)
        weights = jnp.exp(scores - top)
        highest[mine, :] = jnp.broadcast_to(top, (rows, LANES))
        total[mine, :] = jnp.broadcast_to(jnp.sum(weights, axis=1, keepdims=True), (rows, LANES))
        out[mine, :] = jnp.dot(weights.astype(BF16), values[i, 0], preferred_element_type=F32)


def cached_attention(lengths, q, keys, values, per_step=4):
    steps, requests, cols = q.shape
    positions, head_dim = keys.shape[2], keys.shape[3]
    rows = steps * requests * (cols // head_dim)
    cache = pl.BlockSpec((per_step, 1, positions, head_dim), lambda i: (i, 0, 0, 0))
    whole = pl.BlockSpec((rows, LANES), lambda i: (0, 0))
    kernel = lambda *refs: cached_kernel(*refs, scale=1.0 / math.sqrt(head_dim))
    return pl.pallas_call(
        kernel,
        grid=(requests // per_step,),
        out_shape=(jax.ShapeDtypeStruct((rows, LANES), F32),) * 3,
        in_specs=[SMEM, pl.BlockSpec(q.shape, lambda i: (0, 0, 0)), cache, cache],
        out_specs=(whole,) * 3,
        scratch_shapes=[pltpu.VMEM((rows, head_dim), F32)],
        compiler_params=params("arbitrary"),
        cost_estimate=pl.CostEstimate(
            flops=4 * rows * positions * head_dim,
            bytes_accessed=4 * requests * positions * head_dim,
            transcendentals=rows * positions,
        ),
        name="cached",
    )(lengths, q, keys, values)


def owned(row_ids, pair, rank, lane):
    per_vector = LANES // rank
    return row_ids == (lane // rank + pair * per_vector).astype(F32)


def shrink_kernel(received, down, projected, out, total, row_ids):
    step = pl.program_id(0)
    adapters, rank, cols = down.shape
    rows = received.shape[0]
    lane = iota((rows, LANES), 1)
    pairs = adapters * rank // LANES

    @pl.when(step == 0)
    def _():
        total[...] = jnp.zeros_like(total)
        row_ids[...] = received[:, cols:].astype(F32)

    products = contract_last(received[:, :cols], down[...].reshape(adapters * rank, cols))
    kept = total[...]
    for i in range(pairs):
        mask = owned(row_ids[...], step * pairs + i, rank, lane)
        kept = kept + jnp.where(mask, products[:, i * LANES : (i + 1) * LANES], 0.0)
    total[...] = kept

    @pl.when(step == pl.num_programs(0) - 1)
    def _():
        both = kept + pltpu.roll(kept, rank, 1)
        half = rows // 2
        partial = jnp.where(lane[:half] < rank, both[:half], both[half:]).astype(BF16)
        kv_rows = projected.shape[1]
        for t in range(out.shape[0]):
            out[t, :kv_rows] = projected[t]
            out[t, kv_rows:] = partial


def shrink(received, down, projected, per_step=8):
    adapters, rank, cols = down.shape
    rows = received.shape[0]
    heads, kv_rows, head_dim = projected.shape
    fixed = lambda shape: pl.BlockSpec(shape, lambda i: (0,) * len(shape))
    out_shape = (heads, kv_rows + rows // 2, LANES)
    return pl.pallas_call(
        shrink_kernel,
        grid=(adapters // per_step,),
        out_shape=jax.ShapeDtypeStruct(out_shape, BF16),
        in_specs=[
            fixed(received.shape),
            pl.BlockSpec((per_step, rank, cols), lambda i: (i, 0, 0)),
            fixed(projected.shape),
        ],
        out_specs=fixed(out_shape),
        scratch_shapes=[pltpu.VMEM((rows, LANES), F32), pltpu.VMEM((rows, LANES), F32)],
        compiler_params=params("arbitrary"),
        cost_estimate=pl.CostEstimate(
            flops=2 * rows * adapters * rank * cols,
            bytes_accessed=2 * adapters * rank * cols,
            transcendentals=0,
        ),
        name="shrink",
    )(received, down, projected)


def expand_kernel(summands, received, up, new_keys, base_values, correction):
    sources, all_rows, lanes = summands.shape
    adapters, rank, head_dim = up.shape
    rows = received.shape[0]
    half = rows // 2
    tokens = (all_rows - half) // 2
    total = summands[0].astype(F32)
    for t in range(1, sources):
        total = total + summands[t].astype(F32)
    new_keys[...] = total[:tokens].astype(BF16)
    base_values[...] = total[tokens : 2 * tokens]
    packed = total[2 * tokens :]
    turned = pltpu.roll(packed, rank, 1)
    low = iota((half, LANES), 1) < rank
    shrunk = jnp.concatenate(
        [jnp.where(low, packed, turned), jnp.where(low, turned, packed)], axis=0
    )
    row_ids = received[:, received.shape[1] - LANES :].astype(F32)
    lane = iota((rows, LANES), 1)
    pairs = adapters * rank // LANES
    per_vector = LANES // rank
    grown = jnp.zeros((rows, head_dim), F32)
    for i in range(pairs):
        mine = jnp.where(owned(row_ids, i, rank, lane), shrunk, 0.0).astype(BF16)
        block = up[i * per_vector : (i + 1) * per_vector].reshape(LANES, head_dim)
        grown = grown + jnp.dot(mine, block, preferred_element_type=F32)
    correction[...] = grown.astype(BF16)


def expand(summands, received, up):
    sources, all_rows, _ = summands.shape
    rows = received.shape[0]
    tokens = (all_rows - rows // 2) // 2
    head_dim = up.shape[2]
    return pl.pallas_call(
        expand_kernel,
        out_shape=(
            jax.ShapeDtypeStruct((tokens, head_dim), BF16),
            jax.ShapeDtypeStruct((tokens, head_dim), F32),
            jax.ShapeDtypeStruct((rows, head_dim), BF16),
        ),
        in_specs=[VMEM] * 3,
        out_specs=(VMEM,) * 3,
        compiler_params=params(),
        name="expand",
    )(summands, received, up)


def weigh_kernel(q, new_keys, out, highest, total, weights, mixed, *, scale):
    steps, requests, cols = q.shape
    tokens, head_dim = new_keys.shape
    groups = cols // head_dim
    keys = new_keys[...]
    rows = groups * requests
    for s in range(steps):
        q_rows = jnp.concatenate(
            [q[s, :, g * head_dim : (g + 1) * head_dim] for g in range(groups)], axis=0
        )
        scores = contract_last(q_rows, keys) * scale
        row, token = iota((rows, tokens), 0), iota((rows, tokens), 1)
        seen = (token % requests == row % requests) & (token // requests <= s)
        scores = jnp.where(seen, scores, MASKED)
        part = slice(s * rows, (s + 1) * rows)
        cached_top = highest[part, :1]
        top = jnp.maximum(jnp.max(scores, axis=1, keepdims=True), cached_top)
        fresh = jnp.exp(scores - top)
        rescale = jnp.exp(cached_top - top)
        norm = 1.0 / (total[part, :1] * rescale + jnp.sum(fresh, axis=1, keepdims=True))
        weights[part, :] = (fresh * norm).astype(BF16)
        mixed[part, :] = out[part, :] * (rescale * norm)


def weigh(q, new_keys, out, highest, total):
    rows, head_dim = out.shape
    tokens = new_keys.shape[0]
    kernel = lambda *refs: weigh_kernel(*refs, scale=1.0 / math.sqrt(head_dim))
    return pl.pallas_call(
        kernel,
        out_shape=(
            jax.ShapeDtypeStruct((rows, tokens), BF16),
            jax.ShapeDtypeStruct((rows, head_dim), F32),
        ),
        in_specs=[VMEM] * 5,
        out_specs=(VMEM,) * 2,
        compiler_params=params(),
        cost_estimate=pl.CostEstimate(
            flops=4 * rows * tokens * head_dim,
            bytes_accessed=16 * rows * head_dim,
            transcendentals=rows * tokens,
        ),
        name="weigh",
    )(q, new_keys, out, highest, total)


def finish_kernel(returned, slot_of_token, base_values, weights, mixed, values_out, attention):
    steps, requests, cols = attention.shape
    tokens, head_dim = base_values.shape
    slot_rows = returned.shape[0]
    groups = cols // head_dim
    slots = jnp.concatenate([slot_of_token[...]] * (slot_rows // LANES), axis=1)
    token, place = iota((tokens, slot_rows), 0), iota((tokens, slot_rows), 1)
    chosen = (place // steps == slots) & (place % steps == token // requests)
    chosen = jnp.where(chosen, 1.0, 0.0).astype(BF16)
    correction = jnp.dot(chosen, returned[...], preferred_element_type=F32)
    values = (base_values[...] + ADAPTER_SCALE * correction).astype(BF16)
    values_out[...] = values
    rows = groups * requests
    for s in range(steps):
        part = slice(s * rows, (s + 1) * rows)
        fresh = jnp.dot(weights[part, :], values, preferred_element_type=F32)
        result = (mixed[part, :] + fresh).astype(BF16)
        for g in range(groups):
            attention[s, :, g * head_dim : (g + 1) * head_dim] = result[
                g * requests : (g + 1) * requests
            ]


def finish(returned, slot_of_token, base_values, weights, mixed, attention_shape):
    return pl.pallas_call(
        finish_kernel,
        out_shape=(
            jax.ShapeDtypeStruct(base_values.shape, BF16),
            jax.ShapeDtypeStruct(attention_shape, BF16),
        ),
        in_specs=[VMEM] * 5,
        out_specs=(VMEM,) * 2,
        compiler_params=params(),
        name="finish",
    )(returned, slot_of_token, base_values, weights, mixed)


def per_device(
    normed_hidden_rows,
    queries,
    key_weight,
    value_weight,
    adapter_down,
    adapter_up,
    adapter_ids,
    owner_map,
    cache_keys,
    cache_values,
    cache_lengths,
):
    steps, requests, _ = normed_hidden_rows.shape
    owners = lax.axis_size("batch")
    tensor_size = lax.axis_size("tensor")
    exchange = lambda a, axis: lax.all_to_all(a, axis, split_axis=0, concat_axis=0, tiled=True)

    packed, slot_of_token = pack(
        adapter_ids, owner_map, normed_hidden_rows, adapter_down.shape[0], owners
    )
    received = exchange(packed, "batch")
    projected = project(normed_hidden_rows, key_weight, value_weight, tensor_size)
    cached = cached_attention(cache_lengths, queries, cache_keys, cache_values)
    summands = exchange(shrink(received, adapter_down, projected), "tensor")
    new_keys, base_values, correction = expand(summands, received, adapter_up)
    returned = exchange(correction, "batch")
    weights, mixed = weigh(queries, new_keys, *cached)
    values, attention = finish(
        returned, slot_of_token, base_values, weights, mixed, queries.shape
    )
    shape = (steps, requests, new_keys.shape[1])
    return (new_keys.reshape(shape), values.reshape(shape), attention)


def solution(mesh):
    placed = (
        P(None, "batch", "tensor"),
        P(None, "batch", "tensor"),
        P("tensor", None),
        P("tensor", None),
        P("batch", None, "tensor"),
        P("batch", None, "tensor"),
        P("batch"),
        P(),
        P("batch", "tensor", None, None),
        P("batch", "tensor", None, None),
        P("batch"),
    )
    return jax.shard_map(
        per_device,
        mesh=mesh,
        in_specs=placed,
        out_specs=(
            P(None, "batch", "tensor"),
            P(None, "batch", "tensor"),
            P(None, "batch", "tensor"),
        ),
        check_vma=False,
    )
```

time: 217 us -> 70.1 us (0.32)
  the two profiles are of different devices: /device:TPU:0 before, /device:TPU:1 now
where the time goes in v1:
time: 70.1 us; the launch traced here: 69.6 us
  blocking collectives  24.4 us (35%)
  Pallas kernels  14.6 us (21%)
  starting transfers between devices  14.5 us (21%)
  local copies, waits for them, and re-layouts  8.55 us (12%)
  waiting for transfers between devices  6.74 us (10%)
  between operations  0.77 us (1%)
    all_to_all x1, blocking collectives, per_device(): lax.all_to_all(a, axis, split_axis=0, concat_axis=0, tiled=True)  24.4 us
    all_to_all x2, starting transfers between devices, per_device(): lax.all_to_all(a, axis, split_axis=0, concat_axis=0, tiled=True)  14.5 us
    unnamed x26, local copies, waits for them, and re-layouts  8.55 us
    all_to_all x2, waiting for transfers between devices, per_device(): lax.all_to_all(a, axis, split_axis=0, concat_axis=0, tiled=True)  6.74 us
    pallas_call x1, Pallas kernels, cached_attention(): pl.pallas_call(kernel, grid=(requests // per_step,), out_shape=(jax.Shape...  4.91 us
    pallas_call x1, Pallas kernels, project(): pl.pallas_call(project_kernel, grid=(heads,), out_shape=jax.ShapeDtypeStr...  2.96 us
    pallas_call x1, Pallas kernels, shrink(): pl.pallas_call(shrink_kernel, grid=(adapters // per_step,), out_shape=jax...  2.02 us
    pallas_call x1, Pallas kernels, pack(): pl.pallas_call(kernel, out_shape=(jax.ShapeDtypeStruct((slot_rows, cols +...  1.84 us
  transfers between devices with their start and end apart: 2, of which 2 were waited for; matrix products, arithmetic and copies ran while one was open for 0% of the time, Pallas kernels for 12%

profile of v1, /device:TPU:1, one launch (start us, length us, event | category | flops | bytes accessed | tf_op | source)
XLA Modules:
  0.0 69.6 jit_solution(5505314395692832915)
XLA Ops:
  0.6 0.0 copy-start.7
  0.6 0.9 %copy-done.7 = bf16[4,16,1024]{2,1,0:T(8,128)(2,1)S(1)} copy-done((bf16[4,16,1024]{2,1,0:T(8,128)(2,1)S(1)}, bf16[4,16,1024]{2,1,0:T(8,128)(2,1)}, u32[]{:S(2)}) %copy-start.7) | copy-done | bytes 131096
  1.5 0.0 copy-start.10
  1.5 0.7 copy-done.10
  2.2 0.7 copy-done.11
  2.9 1.8 %pack.1 = (bf16[256,1152]{1,0:T(8,128)(2,1)}, s32[64,128]{1,0:T(8,128)S(1)}) custom-call(s32[16]{0:T(128)S(1)} %copy-done.11, s32[1024]{0:T(1024)S(1)} %copy-done.10, bf16[4,16,1024]{2,1,0:T(8,128)(2,1)S(1)} %copy-done.7), custom_call_target="tpu_custom_call" | custom-call | tf_op jit(solution)/shard_map/pack/pallas_call | solution.py:74
  4.7 8.6 %all-to-all-start = ((bf16[32,8,1152]{2,1,0:T(8,128)(2,1)}), bf16[32,8,1152]{2,1,0:T(8,128)(2,1)S(1)}, u32[]{:S(2)}, u32[]{:S(2)}) async-start(bf16[32,8,1152]{2,1,0:T(8,128)(2,1)} %bitcast), calls=%async_computation | async-start | bytes 1179648 | tf_op jit(solution)/shard_map/all_to_all | solution.py:379
  13.3 0.0 copy-start.1
  13.3 1.6 %copy-done.1 = bf16[1024,1024]{1,0:T(8,128)(2,1)S(1)} copy-done((bf16[1024,1024]{1,0:T(8,128)(2,1)S(1)}, bf16[1024,1024]{1,0:T(8,128)(2,1)}, u32[]{:S(2)}) %copy-start.1) | copy-done | bytes 2097176
  14.9 1.6 %copy-done.2 = bf16[1024,1024]{1,0:T(8,128)(2,1)S(1)} copy-done((bf16[1024,1024]{1,0:T(8,128)(2,1)S(1)}, bf16[1024,1024]{1,0:T(8,128)(2,1)}, u32[]{:S(2)}) %copy-start.2) | copy-done | bytes 2097176
  16.5 0.9 %copy-done.8 = bf16[4,16,1024]{2,1,0:T(8,128)(2,1)S(1)} copy-done((bf16[4,16,1024]{2,1,0:T(8,128)(2,1)S(1)}, bf16[4,16,1024]{2,1,0:T(8,128)(2,1)}, u32[]{:S(2)}) %copy-start.8) | copy-done | bytes 131096
  17.4 3.0 %project.1.projected = bf16[8,128,128]{2,1,0:T(8,128)(2,1)S(1)} custom-call(bf16[4,16,1024]{2,1,0:T(8,128)(2,1)S(1)} %copy-done.8, bf16[1024,1024]{1,0:T(8,128)(2,1)S(1)} %copy-done.1, bf16[1024,1024]{1,0:T(8,128)(2,1)S(1)} %copy-done.2), custom_call_target="tpu_custom_call" | custom-call | flops 268435456 | bytes 4194304 | tf_op jit(solution)/shard_map/project/pallas_call | solution.py:100
  20.4 5.2 %all-to-all-done = bf16[32,8,1152]{2,1,0:T(8,128)(2,1)S(1)} async-done(((bf16[32,8,1152]{2,1,0:T(8,128)(2,1)}), bf16[32,8,1152]{2,1,0:T(8,128)(2,1)S(1)}, u32[]{:S(2)}, u32[]{:S(2)}) %all-to-all-start) | async-done | bytes 589856 | tf_op jit(solution)/shard_map/all_to_all | solution.py:379
  25.6 2.2 %copy-done = bf16[32,64,1024]{2,1,0:T(8,128)(2,1)S(1)} copy-done((bf16[32,64,1024]{2,1,0:T(8,128)(2,1)S(1)}, bf16[32,64,1024]{2,1,0:T(8,128)(2,1)}, u32[]{:S(2)}) %copy-start) | copy-done | bytes 4194328
  27.8 2.0 %shrink.1 = bf16[8,256,128]{2,1,0:T(8,128)(2,1)S(1)} custom-call(bf16[256,1152]{1,0:T(8,128)(2,1)S(1)} %bitcast.6, bf16[32,64,1024]{2,1,0:T(8,128)(2,1)S(1)} %copy-done, bf16[8,128,128]{2,1,0:T(8,128)(2,1)S(1)} %project.1.projected), custom_call_target="tpu_custom_call" | custom-call | flops 1073741824 | bytes 4194304 | tf_op jit(solution)/shard_map/shrink/pallas_call | solution.py:211
  29.8 0.0 copy-start.3
  29.8 0.0 copy-start.4
  29.8 0.0 copy-start.6
  29.8 0.0 copy-start.12
  29.8 24.4 %all_to_all.27.summands = bf16[8,256,128]{2,1,0:T(8,128)(2,1)S(1)} all-to-all(bf16[8,256,128]{2,1,0:T(8,128)(2,1)S(1)} %shrink.1), channel_id=1, replica_groups=mesh['batch'=32,'tensor'=8] {'tensor'}, dimensions={0} | all-to-all | bytes 1048576 | tf_op jit(solution)/shard_map/all_to_all | solution.py:379
  54.2 0.0 copy-done.5
  54.2 1.1 %expand.1 = (bf16[64,128]{1,0:T(8,128)(2,1)}, f32[64,128]{1,0:T(8,128)S(1)}, bf16[256,128]{1,0:T(8,128)(2,1)}) custom-call(bf16[8,256,128]{2,1,0:T(8,128)(2,1)S(1)} %all_to_all.27.summands, bf16[256,1152]{1,0:T(8,128)(2,1)S(1)} %bitcast.7, bf16[32,64,128]{2,1,0:T(8,128)(2,1)S(1)} %copy-done.5), custom_call_target="tpu_custom_call" | custom-call | tf_op jit(solution)/shard_map/expand/pallas_call | solution.py:266
  55.4 5.9 %all-to-all-start.2 = ((bf16[32,8,128]{2,1,0:T(8,128)(2,1)}), bf16[32,8,128]{2,1,0:T(8,128)(2,1)S(1)}, u32[]{:S(2)}, u32[]{:S(2)}) async-start(bf16[32,8,128]{2,1,0:T(8,128)(2,1)} %bitcast.3), calls=%async_computation.2 | async-start | bytes 131072 | tf_op jit(solution)/shard_map/all_to_all | solution.py:379
  61.3 0.0 copy-done.3
  61.3 0.0 copy-done.4
  61.3 0.0 copy-done.6
  61.3 0.0 copy-done.12
  61.3 4.9 %cached.1 = (f32[512,128]{1,0:T(8,128)S(1)}, f32[512,128]{1,0:T(8,128)S(1)}, f32[512,128]{1,0:T(8,128)S(1)}) custom-call(s32[16]{0:T(128)S(1)} %copy-done.12, bf16[4,16,1024]{2,1,0:T(8,128)(2,1)S(1)} %copy-done.6, bf16[16,1,256,128]{3,2,1,0:T(8,128)(2,1)S(1)} %copy-done.3, bf16[16,1,256,128]{3,2,1,0:T(8,128)(2,1)S(1)} %copy-done.4), custom_call_target="tpu_custom_call" | custom-call | flops 67108864 | bytes 2097152 | tf_op jit(solution)/shard_map/cached/pallas_call | solution.py:153
  66.2 0.0 copy-done.9
  66.3 0.8 %weigh.1 = (bf16[512,64]{1,0:T(8,128)(2,1)S(1)}, f32[512,128]{1,0:T(8,128)S(1)}) custom-call(bf16[4,16,1024]{2,1,0:T(8,128)(2,1)S(1)} %copy-done.6, bf16[64,128]{1,0:T(8,128)(2,1)S(1)} %copy-done.9, f32[512,128]{1,0:T(8,128)S(1)} %get-tuple-element.20.refs_2_, f32[512,128]{1,0:T(8,128)S(1)} %get-tuple-element.21.refs_3_, ...), custom_call_target="tpu_custom_call" | custom-call | flops 16777216 | bytes 1048576 | tf_op jit(solution)/shard_map/weigh/pallas_call | solution.py:308
  67.1 1.5 %all-to-all-done.2 = bf16[32,8,128]{2,1,0:T(8,128)(2,1)S(1)} async-done(((bf16[32,8,128]{2,1,0:T(8,128)(2,1)}), bf16[32,8,128]{2,1,0:T(8,128)(2,1)S(1)}, u32[]{:S(2)}, u32[]{:S(2)}) %all-to-all-start.2) | async-done | bytes 65568 | tf_op jit(solution)/shard_map/all_to_all | solution.py:379
  68.6 1.0 %finish.1 = (bf16[64,128]{1,0:T(8,128)(2,1)}, bf16[4,16,1024]{2,1,0:T(8,128)(2,1)}) custom-call(bf16[256,128]{1,0:T(8,128)(2,1)S(1)} %bitcast.8, s32[64,128]{1,0:T(8,128)S(1)} %get-tuple-element.18.slot_of_token, f32[64,128]{1,0:T(8,128)S(1)} %get-tuple-element.19.base_values, bf16[512,64]{1,0:T(8,128)(2,1)S(1)} %get-tuple-element.23.weights, ...), custom_call_target="tpu_custom_call" | custom-call | tf_op jit(solution)/shard_map/finish/pallas_call | solution.py:350
  (6 shorter events, 0.0 us)
Async XLA Ops:
  0.6 0.9 %copy-start.7 = (bf16[4,16,1024]{2,1,0:T(8,128)(2,1)S(1)}, bf16[4,16,1024]{2,1,0:T(8,128)(2,1)}, u32[]{:S(2)}) copy-start(bf16[4,16,1024]{2,1,0:T(8,128)(2,1)} %x.1) | copy-start | bytes 393220
  1.5 0.7 copy-start.10
  2.2 0.7 copy-start.11
  4.7 20.8 %all-to-all-start = ((bf16[32,8,1152]{2,1,0:T(8,128)(2,1)}), bf16[32,8,1152]{2,1,0:T(8,128)(2,1)S(1)}, u32[]{:S(2)}, u32[]{:S(2)}) async-start(bf16[32,8,1152]{2,1,0:T(8,128)(2,1)} %bitcast), calls=%async_computation | async-start | bytes 1179648 | tf_op jit(solution)/shard_map/all_to_all | solution.py:379
  13.3 1.6 %copy-start.1 = (bf16[1024,1024]{1,0:T(8,128)(2,1)S(1)}, bf16[1024,1024]{1,0:T(8,128)(2,1)}, u32[]{:S(2)}) copy-start(bf16[1024,1024]{1,0:T(8,128)(2,1)} %key_weight.1) | copy-start | bytes 6291460
  14.9 1.6 %copy-start.2 = (bf16[1024,1024]{1,0:T(8,128)(2,1)S(1)}, bf16[1024,1024]{1,0:T(8,128)(2,1)}, u32[]{:S(2)}) copy-start(bf16[1024,1024]{1,0:T(8,128)(2,1)} %value_weight.1) | copy-start | bytes 6291460
  16.5 0.9 %copy-start.8 = (bf16[4,16,1024]{2,1,0:T(8,128)(2,1)S(1)}, bf16[4,16,1024]{2,1,0:T(8,128)(2,1)}, u32[]{:S(2)}) copy-start(bf16[4,16,1024]{2,1,0:T(8,128)(2,1)} %x.1) | copy-start | bytes 393220
  25.6 2.2 %copy-start = (bf16[32,64,1024]{2,1,0:T(8,128)(2,1)S(1)}, bf16[32,64,1024]{2,1,0:T(8,128)(2,1)}, u32[]{:S(2)}) copy-start(bf16[32,64,1024]{2,1,0:T(8,128)(2,1)} %down.1) | copy-start | bytes 12582916
  27.8 26.5 %copy-start.5 = (bf16[32,64,128]{2,1,0:T(8,128)(2,1)S(1)}, bf16[32,64,128]{2,1,0:T(8,128)(2,1)}, u32[]{:S(2)}) copy-start(bf16[32,64,128]{2,1,0:T(8,128)(2,1)} %up.1) | copy-start | bytes 1572868
  29.8 31.5 %copy-start.3 = (bf16[16,1,256,128]{3,2,1,0:T(8,128)(2,1)S(1)}, bf16[16,1,256,128]{3,2,1,0:T(8,128)(2,1)}, u32[]{:S(2)}) copy-start(bf16[16,1,256,128]{3,2,1,0:T(8,128)(2,1)} %refs_2_.3) | copy-start | bytes 3145732
  29.8 31.5 %copy-start.4 = (bf16[16,1,256,128]{3,2,1,0:T(8,128)(2,1)S(1)}, bf16[16,1,256,128]{3,2,1,0:T(8,128)(2,1)}, u32[]{:S(2)}) copy-start(bf16[16,1,256,128]{3,2,1,0:T(8,128)(2,1)} %refs_3_.1) | copy-start | bytes 3145732
  29.8 31.5 %copy-start.6 = (bf16[4,16,1024]{2,1,0:T(8,128)(2,1)S(1)}, bf16[4,16,1024]{2,1,0:T(8,128)(2,1)}, u32[]{:S(2)}) copy-start(bf16[4,16,1024]{2,1,0:T(8,128)(2,1)} %refs_0_.5) | copy-start | bytes 393220
  29.8 31.5 %copy-start.12 = (s32[16]{0:T(128)S(1)}, s32[16]{0:T(128)}, u32[]{:S(2)}) copy-start(s32[16]{0:T(128)} %refs_0_.4) | copy-start | bytes 196
  55.4 10.9 %copy-start.9 = (bf16[64,128]{1,0:T(8,128)(2,1)S(1)}, bf16[64,128]{1,0:T(8,128)(2,1)}, u32[]{:S(2)}) copy-start(bf16[64,128]{1,0:T(8,128)(2,1)} %get-tuple-element.16.refs_1_) | copy-start | bytes 49156
  55.4 13.2 %all-to-all-start.2 = ((bf16[32,8,128]{2,1,0:T(8,128)(2,1)}), bf16[32,8,128]{2,1,0:T(8,128)(2,1)S(1)}, u32[]{:S(2)}, u32[]{:S(2)}) async-start(bf16[32,8,128]{2,1,0:T(8,128)(2,1)} %bitcast.3), calls=%async_computation.2 | async-start | bytes 131072 | tf_op jit(solution)/shard_map/all_to_all | solution.py:379

commit v2 on v1

v2 whole, which is shorter than its diff:
```python
import math

import jax
import jax.numpy as jnp
from jax import lax
from jax.experimental import pallas as pl
from jax.experimental.pallas import tpu as pltpu
from jax.sharding import PartitionSpec as P

HEADS = 64
KV_HEADS = 8
CAP = 2

ADAPTER_SCALE = 0.5
MASKED = -1e30

F32 = jnp.float32
BF16 = jnp.bfloat16
LANES = 128
VMEM = pl.BlockSpec(memory_space=pltpu.VMEM)
HBM = pl.BlockSpec(memory_space=pltpu.HBM)
ANY = pl.BlockSpec(memory_space=pl.ANY)
SMEM = pl.BlockSpec(memory_space=pltpu.SMEM)


def params(mebibytes=16):
    return pltpu.CompilerParams(vmem_limit_bytes=mebibytes * 1024 * 1024)


def iota(shape, dim):
    return lax.broadcasted_iota(jnp.int32, shape, dim)


def contract_last(a, b):
    return lax.dot_general(a, b, (((1,), (1,)), ((), ())), preferred_element_type=F32)


def pack_kernel(
    ids_in, map_in, x_in, packed, slot_of_token, ids, owner_map, x, counts, sems, *, per_owner
):
    copies = [
        pltpu.make_async_copy(source, target, sems.at[i])
        for i, (source, target) in enumerate(((ids_in, ids), (map_in, owner_map), (x_in, x)))
    ]
    for copy in copies:
        copy.start()
    steps, requests, cols = x.shape
    tokens = steps * requests
    slot_rows = packed.shape[0]
    for o in range(counts.shape[0]):
        counts[o] = 0
    token = iota((tokens, LANES), 0) % requests
    column = iota((1, tokens), 1) % requests
    slot_sub = jnp.zeros((tokens, LANES), jnp.int32)
    row_sub = jnp.zeros((tokens, LANES), jnp.int32)
    slot_lane = jnp.zeros((1, tokens), jnp.int32)
    copies[0].wait()
    copies[1].wait()
    for r in range(requests):
        storage = owner_map[ids[r]]
        owner = storage // per_owner
        rank = counts[owner]
        counts[owner] = rank + 1
        slot = owner * CAP + rank
        slot_sub = jnp.where(token == r, slot, slot_sub)
        row_sub = jnp.where(token == r, storage - owner * per_owner, row_sub)
        slot_lane = jnp.where(column == r, slot, slot_lane)
    slot_of_token[...] = slot_sub
    place = iota((slot_rows, tokens), 0)
    source = iota((slot_rows, tokens), 1)
    chosen = (place // steps == slot_lane) & (place % steps == source // requests)
    chosen = jnp.where(chosen, 1.0, 0.0).astype(BF16)
    packed[:, cols:] = jnp.dot(
        chosen, row_sub.astype(F32).astype(BF16), preferred_element_type=F32
    ).astype(BF16)
    copies[2].wait()
    rows = x[...].reshape(tokens, cols)
    packed[:, :cols] = jnp.dot(chosen, rows, preferred_element_type=F32).astype(BF16)


def pack(adapter_ids, owner_map, x, per_owner, owners):
    steps, requests, cols = x.shape
    slot_rows = owners * CAP * steps
    return pl.pallas_call(
        lambda *refs: pack_kernel(*refs, per_owner=per_owner),
        out_shape=(
            jax.ShapeDtypeStruct((slot_rows, cols + LANES), BF16),
            jax.ShapeDtypeStruct((steps * requests, LANES), jnp.int32),
        ),
        in_specs=[HBM, HBM, HBM],
        out_specs=(VMEM, VMEM),
        scratch_shapes=[
            pltpu.SMEM(adapter_ids.shape, jnp.int32),
            pltpu.SMEM(owner_map.shape, jnp.int32),
            pltpu.VMEM(x.shape, BF16),
            pltpu.SMEM((owners,), jnp.int32),
            pltpu.SemaphoreType.DMA((3,)),
        ],
        compiler_params=params(60),
        name="pack",
    )(adapter_ids, owner_map, x)


def project_kernel(place, x_in, key_in, value_in, kept, given, x, key_weight, value_weight, sems):
    moves = ((x_in, x), (key_in, key_weight), (value_in, value_weight))
    copies = [
        pltpu.make_async_copy(source, target, sems.at[i])
        for i, (source, target) in enumerate(moves)
    ]
    for copy in copies:
        copy.start()
    heads, tokens, head_dim = kept.shape
    copies[0].wait()
    rows = x[...].reshape(tokens, x.shape[2])
    copies[1].wait()
    keys = jnp.dot(rows, key_weight[...], preferred_element_type=F32)
    copies[2].wait()
    values = jnp.dot(rows, value_weight[...], preferred_element_type=F32)
    even = place[0] % 2 == 0
    mine = jnp.where(even, keys, values).astype(BF16)
    other = jnp.where(even, values, keys).astype(BF16)
    for h in range(heads):
        kept[h] = mine[:, h * head_dim : (h + 1) * head_dim]
        given[h] = other[:, h * head_dim : (h + 1) * head_dim]


def project(place, x, key_weight, value_weight, heads):
    steps, requests, cols = x.shape
    tokens = steps * requests
    head_dim = key_weight.shape[1] // heads
    return pl.pallas_call(
        project_kernel,
        out_shape=(jax.ShapeDtypeStruct((heads, tokens, head_dim), BF16),) * 2,
        in_specs=[SMEM] + [HBM] * 3,
        out_specs=(VMEM,) * 2,
        scratch_shapes=[pltpu.VMEM(a.shape, BF16) for a in (x, key_weight, value_weight)]
        + [pltpu.SemaphoreType.DMA((3,))],
        compiler_params=params(60),
        cost_estimate=pl.CostEstimate(
            flops=4 * tokens * cols * heads * head_dim,
            bytes_accessed=4 * cols * heads * head_dim,
            transcendentals=0,
        ),
        name="project",
    )(place, x, key_weight, value_weight)


def pair_kernel(kept, taken, out):
    out[...] = (kept[...].astype(F32) + taken[...].astype(F32)).astype(BF16)


def pair(kept, taken):
    return pl.pallas_call(
        pair_kernel,
        out_shape=jax.ShapeDtypeStruct(kept.shape, BF16),
        in_specs=[VMEM] * 2,
        out_specs=VMEM,
        compiler_params=params(),
        name="pair",
    )(kept, taken)


def cached_kernel(
    lengths, after, q_in, cache_keys, cache_values, out, norms,
    q, keys, values, q_rows, scores, weights, sems, *, scale
):
    moves = ((q_in, q), (cache_keys, keys), (cache_values, values))
    copies = [
        pltpu.make_async_copy(source, target, sems.at[i])
        for i, (source, target) in enumerate(moves)
    ]
    for copy in copies:
        copy.start()
    steps, requests, cols = q.shape
    positions, head_dim = keys.shape[2], keys.shape[3]
    groups = cols // head_dim
    rows = steps * groups
    copies[0].wait()
    for s in range(steps):
        for g in range(groups):
            start = (s * groups + g) * requests
            q_rows[start : start + requests] = q[s, :, g * head_dim : (g + 1) * head_dim].astype(
                F32
            )
    copies[1].wait()
    position = iota((rows, positions), 1)
    low = iota((rows, LANES), 1) < LANES // 2
    for r in range(requests):
        mine = pl.ds(r, rows, stride=requests)
        product = contract_last(q_rows[mine, :].astype(BF16), keys[r, 0]) * scale
        scores[r] = jnp.where(position < lengths[r], product, MASKED)
    for r in range(requests):
        mine = pl.ds(r, rows, stride=requests)
        top = jnp.max(scores[r], axis=1, keepdims=True)
        exponent = jnp.exp(scores[r] - top)
        weights[r] = exponent.astype(BF16)
        norms[mine, :] = jnp.where(low, top, jnp.sum(exponent, axis=1, keepdims=True))
    copies[2].wait()
    for r in range(requests):
        mine = pl.ds(r, rows, stride=requests)
        out[mine, :] = jnp.dot(weights[r], values[r, 0], preferred_element_type=F32)


def cached_attention(lengths, after, q, cache_keys, cache_values):
    steps, requests, cols = q.shape
    positions, head_dim = cache_keys.shape[2], cache_keys.shape[3]
    rows = steps * requests * (cols // head_dim)
    return pl.pallas_call(
        lambda *refs: cached_kernel(*refs, scale=1.0 / math.sqrt(head_dim)),
        out_shape=(jax.ShapeDtypeStruct((rows, LANES), F32),) * 2,
        in_specs=[SMEM, ANY] + [HBM] * 3,
        out_specs=(VMEM,) * 2,
        scratch_shapes=[pltpu.VMEM(a.shape, BF16) for a in (q, cache_keys, cache_values)]
        + [
            pltpu.VMEM((rows, head_dim), F32),
            pltpu.VMEM((requests, rows // requests, positions), F32),
            pltpu.VMEM((requests, rows // requests, positions), BF16),
            pltpu.SemaphoreType.DMA((3,)),
        ],
        compiler_params=params(),
        cost_estimate=pl.CostEstimate(
            flops=4 * rows * positions * head_dim,
            bytes_accessed=4 * requests * positions * head_dim,
            transcendentals=rows * positions,
        ),
        name="cached",
    )(lengths, after, q, cache_keys, cache_values)


def shrink_kernel(received, down, partials, out, ids):
    adapters, rank, cols = down.shape
    rows = received.shape[0]
    per_part = 8
    ids[...] = received[:, cols:]
    wide = jnp.concatenate([ids[...].astype(F32)] * (rows // LANES), axis=1)
    diagonal = iota((rows, rows), 0) == iota((rows, rows), 1)
    adapter = jnp.sum(jnp.where(diagonal, wide, 0.0), axis=0, keepdims=True)
    partial = jnp.zeros((rank, rows), F32)
    for first in range(0, adapters, per_part):
        block = down[first : first + per_part].reshape(per_part * rank, cols)
        products = contract_last(block, received[:, :cols])
        for i in range(per_part):
            mine = adapter == float(first + i)
            partial = jnp.where(mine, products[i * rank : (i + 1) * rank], partial)
    partial = partial.astype(BF16)
    tokens = partials.shape[1]
    for t in range(out.shape[0]):
        out[t, :tokens] = partials[t]
        for i in range(rows // LANES):
            start = tokens + i * rank
            out[t, start : start + rank] = partial[:, i * LANES : (i + 1) * LANES]


def shrink(received, down, partials):
    adapters, rank, cols = down.shape
    rows = received.shape[0]
    heads, tokens, _ = partials.shape
    return pl.pallas_call(
        shrink_kernel,
        out_shape=(
            jax.ShapeDtypeStruct((heads, tokens + rank * rows // LANES, LANES), BF16),
            jax.ShapeDtypeStruct((rows, LANES), BF16),
        ),
        in_specs=[VMEM] * 3,
        out_specs=(VMEM,) * 2,
        compiler_params=params(),
        cost_estimate=pl.CostEstimate(
            flops=2 * rows * adapters * rank * cols,
            bytes_accessed=2 * adapters * rank * cols,
            transcendentals=0,
        ),
        name="shrink",
    )(received, down, partials)


def lane_keys(row_ids, rank):
    return row_ids.astype(F32) - (iota(row_ids.shape, 1) // rank).astype(F32)


def expand_kernel(
    after, summands, ids, up, new_keys, keys_again, base_values, correction
):
    sources, all_rows, lanes = summands.shape
    adapters, rank, head_dim = up.shape
    rows = ids.shape[0]
    half = rows // 2
    tokens = all_rows - rank * rows // lanes
    add = lambda parts: sum((part.astype(F32) for part in parts[1:]), parts[0].astype(F32))
    fresh = add([summands[t, :tokens] for t in range(0, sources, 2)]).astype(BF16)
    new_keys[...] = fresh
    keys_again[...] = fresh
    base_values[...] = add([summands[t, :tokens] for t in range(1, sources, 2)])
    packed = add([summands[t, tokens:] for t in range(sources)]).T
    turned = pltpu.roll(packed, rank, 1)
    low = iota((half, LANES), 1) < rank
    shrunk = jnp.concatenate(
        [jnp.where(low, packed, turned), jnp.where(low, turned, packed)], axis=0
    )
    keys = lane_keys(ids[...], rank)
    per_vector = LANES // rank
    grown = jnp.zeros((rows, head_dim), F32)
    for first in range(0, adapters, per_vector):
        mine = jnp.where(keys == float(first), shrunk, 0.0).astype(BF16)
        block = up[first : first + per_vector].reshape(LANES, head_dim)
        grown = grown + jnp.dot(mine, block, preferred_element_type=F32)
    correction[...] = grown.astype(BF16)


def expand(after, summands, ids, up):
    sources, all_rows, lanes = summands.shape
    rows = ids.shape[0]
    _, rank, head_dim = up.shape
    tokens = all_rows - rank * rows // lanes
    return pl.pallas_call(
        expand_kernel,
        out_shape=(
            jax.ShapeDtypeStruct((tokens, head_dim), BF16),
            jax.ShapeDtypeStruct((tokens, head_dim), BF16),
            jax.ShapeDtypeStruct((tokens, head_dim), F32),
            jax.ShapeDtypeStruct((rows, head_dim), BF16),
        ),
        in_specs=[ANY] + [VMEM] * 3,
        out_specs=(VMEM,) * 4,
        compiler_params=params(),
        name="expand",
    )(after, summands, ids, up)


def weigh_kernel(q, new_keys, out, norms, slot_of_token, weights, mixed, chosen, *, scale):
    steps, requests, cols = q.shape
    tokens, head_dim = new_keys.shape
    slot_rows = chosen.shape[1]
    slots = jnp.concatenate([slot_of_token[...]] * (slot_rows // LANES), axis=1)
    token, place = iota((tokens, slot_rows), 0), iota((tokens, slot_rows), 1)
    found = (place // steps == slots) & (place % steps == token // requests)
    chosen[...] = jnp.where(found, 1.0, 0.0).astype(BF16)
    groups = cols // head_dim
    keys = new_keys[...]
    rows = groups * requests
    for s in range(steps):
        q_rows = jnp.concatenate(
            [q[s, :, g * head_dim : (g + 1) * head_dim] for g in range(groups)], axis=0
        )
        scores = contract_last(q_rows, keys) * scale
        row, token = iota((rows, tokens), 0), iota((rows, tokens), 1)
        seen = (token % requests == row % requests) & (token // requests <= s)
        scores = jnp.where(seen, scores, MASKED)
        part = slice(s * rows, (s + 1) * rows)
        cached_top = norms[part, :1]
        cached_sum = norms[part, LANES // 2 : LANES // 2 + 1]
        top = jnp.maximum(jnp.max(scores, axis=1, keepdims=True), cached_top)
        fresh = jnp.exp(scores - top)
        rescale = jnp.exp(cached_top - top)
        norm = 1.0 / (cached_sum * rescale + jnp.sum(fresh, axis=1, keepdims=True))
        weights[part, :] = (fresh * norm).astype(BF16)
        mixed[part, :] = out[part, :] * (rescale * norm)


def weigh(q, new_keys, out, norms, slot_of_token, slot_rows):
    rows, head_dim = out.shape
    tokens = new_keys.shape[0]
    kernel = lambda *refs: weigh_kernel(*refs, scale=1.0 / math.sqrt(head_dim))
    return pl.pallas_call(
        kernel,
        out_shape=(
            jax.ShapeDtypeStruct((rows, tokens), BF16),
            jax.ShapeDtypeStruct((rows, head_dim), F32),
            jax.ShapeDtypeStruct((tokens, slot_rows), BF16),
        ),
        in_specs=[VMEM] * 5,
        out_specs=(VMEM,) * 3,
        compiler_params=params(),
        cost_estimate=pl.CostEstimate(
            flops=4 * rows * tokens * head_dim,
            bytes_accessed=16 * rows * head_dim,
            transcendentals=rows * tokens,
        ),
        name="weigh",
    )(q, new_keys, out, norms, slot_of_token)


def finish_kernel(returned, chosen, base_values, weights, mixed, values_out, attention):
    steps, requests, cols = attention.shape
    tokens, head_dim = base_values.shape
    groups = cols // head_dim
    correction = jnp.dot(chosen[...], returned[...], preferred_element_type=F32)
    values = (base_values[...] + ADAPTER_SCALE * correction).astype(BF16)
    values_out[...] = values
    rows = groups * requests
    for s in range(steps):
        part = slice(s * rows, (s + 1) * rows)
        fresh = jnp.dot(weights[part, :], values, preferred_element_type=F32)
        result = (mixed[part, :] + fresh).astype(BF16)
        for g in range(groups):
            attention[s, :, g * head_dim : (g + 1) * head_dim] = result[
                g * requests : (g + 1) * requests
            ]


def finish(returned, chosen, base_values, weights, mixed, attention_shape):
    return pl.pallas_call(
        finish_kernel,
        out_shape=(
            jax.ShapeDtypeStruct(base_values.shape, BF16),
            jax.ShapeDtypeStruct(attention_shape, BF16),
        ),
        in_specs=[VMEM] * 5,
        out_specs=(VMEM,) * 2,
        compiler_params=params(),
        name="finish",
    )(returned, chosen, base_values, weights, mixed)


def per_device(
    normed_hidden_rows,
    queries,
    key_weight,
    value_weight,
    adapter_down,
    adapter_up,
    adapter_ids,
    owner_map,
    cache_keys,
    cache_values,
    cache_lengths,
):
    steps, requests, _ = normed_hidden_rows.shape
    owners = lax.axis_size("batch")
    tensor_size = lax.axis_size("tensor")
    exchange = lambda a, axis: lax.all_to_all(a, axis, split_axis=0, concat_axis=0, tiled=True)

    packed, slot_of_token = pack(
        adapter_ids, owner_map, normed_hidden_rows, adapter_down.shape[0], owners
    )
    received = exchange(packed, "batch")
    place = lax.axis_index("tensor")[None]
    kept, given = project(place, normed_hidden_rows, key_weight, value_weight, tensor_size)
    neighbours = [(i, i ^ 1) for i in range(tensor_size)]
    taken = lax.ppermute(given, "tensor", neighbours)
    summands, ids = shrink(received, adapter_down, pair(kept, taken))
    cached = cached_attention(cache_lengths, summands, queries, cache_keys, cache_values)
    summands = exchange(summands, "tensor")
    new_keys, fresh_keys, base_values, correction = expand(cached[0], summands, ids, adapter_up)
    returned = exchange(correction, "batch")
    weights, mixed, chosen = weigh(
        queries, fresh_keys, *cached, slot_of_token, correction.shape[0]
    )
    values, attention = finish(returned, chosen, base_values, weights, mixed, queries.shape)
    shape = (steps, requests, new_keys.shape[1])
    return (new_keys.reshape(shape), values.reshape(shape), attention)


def solution(mesh):
    placed = (
        P(None, "batch", "tensor"),
        P(None, "batch", "tensor"),
        P("tensor", None),
        P("tensor", None),
        P("batch", None, "tensor"),
        P("batch", None, "tensor"),
        P("batch"),
        P(),
        P("batch", "tensor", None, None),
        P("batch", "tensor", None, None),
        P("batch"),
    )
    return jax.shard_map(
        per_device,
        mesh=mesh,
        in_specs=placed,
        out_specs=(
            P(None, "batch", "tensor"),
            P(None, "batch", "tensor"),
            P(None, "batch", "tensor"),
        ),
        check_vma=False,
    )
```

time: 70.1 us -> 66.1 us (0.943)
  blocking collectives: 24.4 us -> 0 us
  waiting for transfers between devices: 6.74 us -> 22.3 us
  starting transfers between devices: 14.5 us -> 23.5 us
  local copies, waits for them, and re-layouts: 8.55 us -> 6.41 us
  Pallas kernels: 14.6 us -> 12.6 us
    all_to_all x1 -> x0, blocking collectives: 24.4 us -> none  [per_device(): lax.all_to_all(a, axis, split_axis=0, concat_axis=0, tiled=True)]
    all_to_all x2 -> x3, waiting for transfers between devices: 6.74 us -> 18.5 us  [per_device(): lax.all_to_all(a, axis, split_axis=0, concat_axis=0, tiled=True)]
    all_to_all x2 -> x3, starting transfers between devices: 14.5 us -> 21.8 us  [per_device(): lax.all_to_all(a, axis, split_axis=0, concat_axis=0, tiled=True)]
    ppermute x0 -> x1, waiting for transfers between devices: none -> 3.82 us  [per_device(): taken = lax.ppermute(given, 'tensor', neighbours)]
    pallas_call x4 -> x5, Pallas kernels: 11.7 us -> 9.55 us  [the longest x1 3.51 us: project(): pl.pallas_call(project_kernel, out_shape=(jax.ShapeDtypeStruct((heads, to...]
    unnamed x26 -> x20, local copies, waits for them, and re-layouts: 8.55 us -> 6.41 us
    ppermute x0 -> x1, starting transfers between devices: none -> 1.73 us  [per_device(): taken = lax.ppermute(given, 'tensor', neighbours)]
  transfers between devices with their start and end apart: 2 -> 4, of which waited for: 2 -> 4; matrix products, arithmetic and copies ran while one was open for 0% -> 0% of each run, Pallas kernels for 12% -> 10%
where the time goes in v2:
time: 66.1 us; the launch traced here: 65.6 us
  starting transfers between devices  23.5 us (36%)
  waiting for transfers between devices  22.3 us (34%)
  Pallas kernels  12.6 us (19%)
  local copies, waits for them, and re-layouts  6.41 us (10%)
  between operations  0.73 us (1%)
    all_to_all x3, starting transfers between devices, per_device(): lax.all_to_all(a, axis, split_axis=0, concat_axis=0, tiled=True)  21.8 us
    all_to_all x3, waiting for transfers between devices, per_device(): lax.all_to_all(a, axis, split_axis=0, concat_axis=0, tiled=True)  18.5 us
    unnamed x20, local copies, waits for them, and re-layouts  6.41 us
    ppermute x1, waiting for transfers between devices, per_device(): taken = lax.ppermute(given, 'tensor', neighbours)  3.82 us
    pallas_call x1, Pallas kernels, project(): pl.pallas_call(project_kernel, out_shape=(jax.ShapeDtypeStruct((heads, to...  3.51 us
    pallas_call x1, Pallas kernels, pack(): pl.pallas_call(lambda *refs: pack_kernel(*refs, per_owner=per_owner), out...  2.12 us
    pallas_call x1, Pallas kernels, shrink(): pl.pallas_call(shrink_kernel, out_shape=(jax.ShapeDtypeStruct((heads, tok...  2.06 us
    pallas_call x1, Pallas kernels, cached_attention(): pl.pallas_call(lambda *refs: cached_kernel(*refs, scale=1.0 / math.sqrt(h...  1.82 us
  transfers between devices with their start and end apart: 4, of which 4 were waited for; matrix products, arithmetic and copies ran while one was open for 0% of the time, Pallas kernels for 10%

profile of v2, /device:TPU:1, one launch (start us, length us, event | category | flops | bytes accessed | tf_op | source)
XLA Modules:
  0.0 65.6 jit_solution(3121099843157429691)
XLA Ops:
  0.6 2.1 %pack.1 = (bf16[256,1152]{1,0:T(8,128)(2,1)}, s32[64,128]{1,0:T(8,128)}) custom-call(s32[16]{0:T(128)} %refs_0_.3, s32[1024]{0:T(1024)} %refs_1_.1, bf16[4,16,1024]{2,1,0:T(8,128)(2,1)} %x_in.1), custom_call_target="tpu_custom_call" | custom-call | tf_op jit(solution)/shard_map/pack/pallas_call | solution.py:84
  2.8 8.6 %all-to-all-start = ((bf16[32,8,1152]{2,1,0:T(8,128)(2,1)}), bf16[32,8,1152]{2,1,0:T(8,128)(2,1)S(1)}, u32[]{:S(2)}, u32[]{:S(2)}) async-start(bf16[32,8,1152]{2,1,0:T(8,128)(2,1)} %bitcast.9), calls=%async_computation | async-start | bytes 1179648 | tf_op jit(solution)/shard_map/all_to_all | solution.py:430
  11.4 3.5 %project.1 = (bf16[8,64,128]{2,1,0:T(8,128)(2,1)}, bf16[8,64,128]{2,1,0:T(8,128)(2,1)}) custom-call(s32[1]{0:T(128)} %bitcast.2.place, bf16[4,16,1024]{2,1,0:T(8,128)(2,1)} %x_in.1, bf16[1024,1024]{1,0:T(8,128)(2,1)} %key_in.1, bf16[1024,1024]{1,0:T(8,128)(2,1)} %value_in.1), custom_call_target="tpu_custom_call" | custom-call | flops 268435456 | bytes 4194304 | tf_op jit(solution)/shard_map/project/pallas_call | solution.py:131
  14.9 1.7 %collective-permute-start = (bf16[8,64,128]{2,1,0:T(8,128)(2,1)}, bf16[8,64,128]{2,1,0:T(8,128)(2,1)S(1)}, u32[]{:S(2)}, u32[]{:S(2)}) collective-permute-start(bf16[8,64,128]{2,1,0:T(8,128)(2,1)} %get-tuple-element.22), channel_id=1, source_target_pairs={{0,1},{1,0},{2,3},{3,2},{4,5},{5,4},{6,7},{7,6},{8,9},{9,8},{10,11... | collective-permute-start | bytes 393224 | tf_op jit(solution)/shard_map/ppermute | solution.py:439
  16.6 3.8 %collective-permute-done.taken = bf16[8,64,128]{2,1,0:T(8,128)(2,1)S(1)} collective-permute-done((bf16[8,64,128]{2,1,0:T(8,128)(2,1)}, bf16[8,64,128]{2,1,0:T(8,128)(2,1)S(1)}, u32[]{:S(2)}, u32[]{:S(2)}) %collective-permute-start) | collective-permute-done | bytes 131104 | tf_op jit(solution)/shard_map/ppermute | solution.py:439
  20.4 0.0 copy-start.7
  20.4 0.9 %copy-done.7 = bf16[8,64,128]{2,1,0:T(8,128)(2,1)S(1)} copy-done((bf16[8,64,128]{2,1,0:T(8,128)(2,1)S(1)}, bf16[8,64,128]{2,1,0:T(8,128)(2,1)}, u32[]{:S(2)}) %copy-start.7) | copy-done | bytes 131096
  21.4 2.2 %all-to-all-done = bf16[32,8,1152]{2,1,0:T(8,128)(2,1)S(1)} async-done(((bf16[32,8,1152]{2,1,0:T(8,128)(2,1)}), bf16[32,8,1152]{2,1,0:T(8,128)(2,1)S(1)}, u32[]{:S(2)}, u32[]{:S(2)}) %all-to-all-start) | async-done | bytes 589856 | tf_op jit(solution)/shard_map/all_to_all | solution.py:430
  23.6 2.2 %copy-done = bf16[32,64,1024]{2,1,0:T(8,128)(2,1)S(1)} copy-done((bf16[32,64,1024]{2,1,0:T(8,128)(2,1)S(1)}, bf16[32,64,1024]{2,1,0:T(8,128)(2,1)}, u32[]{:S(2)}) %copy-start) | copy-done | bytes 4194328
  25.8 0.0 copy-start.1
  25.8 0.0 copy-start.2
  25.8 0.0 copy-start.9
  25.8 2.1 %shrink.1 = (bf16[8,192,128]{2,1,0:T(8,128)(2,1)}, bf16[256,128]{1,0:T(8,128)(2,1)S(1)}) custom-call(bf16[256,1152]{1,0:T(8,128)(2,1)S(1)} %bitcast.7, bf16[32,64,1024]{2,1,0:T(8,128)(2,1)S(1)} %copy-done, bf16[8,64,128]{2,1,0:T(8,128)(2,1)S(1)} %pair.1.partials), custom_call_target="tpu_custom_call" | custom-call | flops 1073741824 | bytes 4194304 | tf_op jit(solution)/shard_map/shrink/pallas_call | solution.py:258
  27.9 8.3 %all-to-all-start.1 = ((bf16[8,192,128]{2,1,0:T(8,128)(2,1)}), bf16[8,192,128]{2,1,0:T(8,128)(2,1)S(1)}, u32[]{:S(2)}, u32[]{:S(2)}) async-start(bf16[8,192,128]{2,1,0:T(8,128)(2,1)} %get-tuple-element.23.refs_1_), calls=%async_computation.1 | async-start | bytes 786432 | tf_op jit(solution)/shard_map/all_to_all | solution.py:430
  36.2 0.0 copy-done.1
  36.2 0.0 copy-done.2
  36.2 0.0 copy-done.9
  36.2 0.0 copy-start.4
  36.2 0.9 %copy-done.4 = bf16[4,16,1024]{2,1,0:T(8,128)(2,1)S(1)} copy-done((bf16[4,16,1024]{2,1,0:T(8,128)(2,1)S(1)}, bf16[4,16,1024]{2,1,0:T(8,128)(2,1)}, u32[]{:S(2)}) %copy-start.4) | copy-done | bytes 131096
  37.1 1.8 %cached.1 = (f32[512,128]{1,0:T(8,128)S(1)}, f32[512,128]{1,0:T(8,128)S(1)}) custom-call(s32[16]{0:T(128)S(1)} %copy-done.9, bf16[8,192,128]{2,1,0:T(8,128)(2,1)} %get-tuple-element.23.refs_1_, bf16[4,16,1024]{2,1,0:T(8,128)(2,1)S(1)} %copy-done.4, bf16[16,1,256,128]{3,2,1,0:T(8,128)(2,1)S(1)} %copy-done.1, bf16[16,1,256,128]{3,2,1,0:T(8,128)(2,1)S(1)} %copy-done.2), custom_call_target="tpu_custom_call" | custom-call | flops 67108864 | bytes 2097152 | tf_op jit(solution)/shard_map/cached/pallas_call | solution.py:208
  39.0 0.0 copy-start.5
  39.0 0.7 %copy-done.5 = f32[512,128]{1,0:T(8,128)} copy-done((f32[512,128]{1,0:T(8,128)}, f32[512,128]{1,0:T(8,128)S(1)}, u32[]{:S(2)}) %copy-start.5) | copy-done | bytes 262168
  39.7 11.6 %all-to-all-done.1.summands = bf16[8,192,128]{2,1,0:T(8,128)(2,1)S(1)} async-done(((bf16[8,192,128]{2,1,0:T(8,128)(2,1)}), bf16[8,192,128]{2,1,0:T(8,128)(2,1)S(1)}, u32[]{:S(2)}, u32[]{:S(2)}) %all-to-all-start.1) | async-done | bytes 393248 | tf_op jit(solution)/shard_map/all_to_all | solution.py:430
  51.2 0.0 copy-done.3
  51.2 1.2 %expand.1 = (bf16[64,128]{1,0:T(8,128)(2,1)}, bf16[64,128]{1,0:T(8,128)(2,1)S(1)}, f32[64,128]{1,0:T(8,128)S(1)}, bf16[256,128]{1,0:T(8,128)(2,1)}) custom-call(f32[512,128]{1,0:T(8,128)S(1)} %get-tuple-element.24.after.refs_2_, bf16[8,192,128]{2,1,0:T(8,128)(2,1)S(1)} %all-to-all-done.1.summands, bf16[256,128]{1,0:T(8,128)(2,1)S(1)} %get-tuple-element.25.ids, ...), custom_call_target="tpu_custom_call" | custom-call | tf_op jit(solution)/shard_map/expand/pallas_call | solution.py:314
  52.4 4.9 %all-to-all-start.2 = ((bf16[32,8,128]{2,1,0:T(8,128)(2,1)}), bf16[32,8,128]{2,1,0:T(8,128)(2,1)S(1)}, u32[]{:S(2)}, u32[]{:S(2)}) async-start(bf16[32,8,128]{2,1,0:T(8,128)(2,1)} %bitcast.4), calls=%async_computation.2 | async-start | bytes 131072 | tf_op jit(solution)/shard_map/all_to_all | solution.py:430
  57.3 0.0 copy-start.6
  57.3 0.9 %copy-done.6 = f32[512,128]{1,0:T(8,128)S(1)} copy-done((f32[512,128]{1,0:T(8,128)S(1)}, f32[512,128]{1,0:T(8,128)}, u32[]{:S(2)}) %copy-start.6) | copy-done | bytes 262168
  58.3 0.8 %copy-done.8 = s32[64,128]{1,0:T(8,128)S(1)} copy-done((s32[64,128]{1,0:T(8,128)S(1)}, s32[64,128]{1,0:T(8,128)}, u32[]{:S(2)}) %copy-start.8) | copy-done | bytes 32792
  59.0 0.9 %weigh.1 = (bf16[512,64]{1,0:T(8,128)(2,1)S(1)}, f32[512,128]{1,0:T(8,128)S(1)}, bf16[64,256]{1,0:T(8,128)(2,1)S(1)}) custom-call(bf16[4,16,1024]{2,1,0:T(8,128)(2,1)S(1)} %copy-done.4, bf16[64,128]{1,0:T(8,128)(2,1)S(1)} %get-tuple-element.28.refs_1_, f32[512,128]{1,0:T(8,128)S(1)} %get-tuple-element.24.after.refs_2_, f32[512,128]{1,0:T(8,128)S(1)} %copy-done.6, ...), custom_call_target="tpu_custom_call" | custom-call | flops 16777216 | bytes 1048576 | tf_op jit(solution)/shard_map/weigh/pallas_call | solution.py:363
  60.0 4.7 %all-to-all-done.2 = bf16[32,8,128]{2,1,0:T(8,128)(2,1)S(1)} async-done(((bf16[32,8,128]{2,1,0:T(8,128)(2,1)}), bf16[32,8,128]{2,1,0:T(8,128)(2,1)S(1)}, u32[]{:S(2)}, u32[]{:S(2)}) %all-to-all-start.2) | async-done | bytes 65568 | tf_op jit(solution)/shard_map/all_to_all | solution.py:430
  64.7 1.0 %finish.1 = (bf16[64,128]{1,0:T(8,128)(2,1)}, bf16[4,16,1024]{2,1,0:T(8,128)(2,1)}) custom-call(bf16[256,128]{1,0:T(8,128)(2,1)S(1)} %bitcast.8, bf16[64,256]{1,0:T(8,128)(2,1)S(1)} %get-tuple-element.31.chosen, f32[64,128]{1,0:T(8,128)S(1)} %get-tuple-element.32.base_values, bf16[512,64]{1,0:T(8,128)(2,1)S(1)} %get-tuple-element.33.weights, ...), custom_call_target="tpu_custom_call" | custom-call | tf_op jit(solution)/shard_map/finish/pallas_call | solution.py:401
  (4 shorter events, 0.0 us)
Async XLA Ops:
  2.8 20.9 %all-to-all-start = ((bf16[32,8,1152]{2,1,0:T(8,128)(2,1)}), bf16[32,8,1152]{2,1,0:T(8,128)(2,1)S(1)}, u32[]{:S(2)}, u32[]{:S(2)}) async-start(bf16[32,8,1152]{2,1,0:T(8,128)(2,1)} %bitcast.9), calls=%async_computation | async-start | bytes 1179648 | tf_op jit(solution)/shard_map/all_to_all | solution.py:430
  14.9 5.6 %collective-permute-start = (bf16[8,64,128]{2,1,0:T(8,128)(2,1)}, bf16[8,64,128]{2,1,0:T(8,128)(2,1)S(1)}, u32[]{:S(2)}, u32[]{:S(2)}) collective-permute-start(bf16[8,64,128]{2,1,0:T(8,128)(2,1)} %get-tuple-element.22), channel_id=1, source_target_pairs={{0,1},{1,0},{2,3},{3,2},{4,5},{5,4},{6,7},{7,6},{8,9},{9,8},{10,11... | collective-permute-start | bytes 393224 | tf_op jit(solution)/shard_map/ppermute | solution.py:439
  20.4 0.9 %copy-start.7 = (bf16[8,64,128]{2,1,0:T(8,128)(2,1)S(1)}, bf16[8,64,128]{2,1,0:T(8,128)(2,1)}, u32[]{:S(2)}) copy-start(bf16[8,64,128]{2,1,0:T(8,128)(2,1)} %get-tuple-element.21.kept) | copy-start | bytes 393220
  23.6 2.2 %copy-start = (bf16[32,64,1024]{2,1,0:T(8,128)(2,1)S(1)}, bf16[32,64,1024]{2,1,0:T(8,128)(2,1)}, u32[]{:S(2)}) copy-start(bf16[32,64,1024]{2,1,0:T(8,128)(2,1)} %down.1) | copy-start | bytes 12582916
  25.8 10.4 %copy-start.1 = (bf16[16,1,256,128]{3,2,1,0:T(8,128)(2,1)S(1)}, bf16[16,1,256,128]{3,2,1,0:T(8,128)(2,1)}, u32[]{:S(2)}) copy-start(bf16[16,1,256,128]{3,2,1,0:T(8,128)(2,1)} %refs_3_.1) | copy-start | bytes 3145732
  25.8 10.4 %copy-start.2 = (bf16[16,1,256,128]{3,2,1,0:T(8,128)(2,1)S(1)}, bf16[16,1,256,128]{3,2,1,0:T(8,128)(2,1)}, u32[]{:S(2)}) copy-start(bf16[16,1,256,128]{3,2,1,0:T(8,128)(2,1)} %refs_4_.1) | copy-start | bytes 3145732
  25.8 10.4 %copy-start.9 = (s32[16]{0:T(128)S(1)}, s32[16]{0:T(128)}, u32[]{:S(2)}) copy-start(s32[16]{0:T(128)} %refs_0_.4) | copy-start | bytes 196
  27.9 23.4 %copy-start.3 = (bf16[32,64,128]{2,1,0:T(8,128)(2,1)S(1)}, bf16[32,64,128]{2,1,0:T(8,128)(2,1)}, u32[]{:S(2)}) copy-start(bf16[32,64,128]{2,1,0:T(8,128)(2,1)} %up.1) | copy-start | bytes 1572868
  27.9 23.4 %all-to-all-start.1 = ((bf16[8,192,128]{2,1,0:T(8,128)(2,1)}), bf16[8,192,128]{2,1,0:T(8,128)(2,1)S(1)}, u32[]{:S(2)}, u32[]{:S(2)}) async-start(bf16[8,192,128]{2,1,0:T(8,128)(2,1)} %get-tuple-element.23.refs_1_), calls=%async_computation.1 | async-start | bytes 786432 | tf_op jit(solution)/shard_map/all_to_all | solution.py:430
  36.2 0.9 %copy-start.4 = (bf16[4,16,1024]{2,1,0:T(8,128)(2,1)S(1)}, bf16[4,16,1024]{2,1,0:T(8,128)(2,1)}, u32[]{:S(2)}) copy-start(bf16[4,16,1024]{2,1,0:T(8,128)(2,1)} %refs_0_.5) | copy-start | bytes 393220
  39.0 0.7 %copy-start.5 = (f32[512,128]{1,0:T(8,128)}, f32[512,128]{1,0:T(8,128)S(1)}, u32[]{:S(2)}) copy-start(f32[512,128]{1,0:T(8,128)S(1)} %get-tuple-element.29.refs_3_) | copy-start | bytes 786436
  52.4 12.2 %all-to-all-start.2 = ((bf16[32,8,128]{2,1,0:T(8,128)(2,1)}), bf16[32,8,128]{2,1,0:T(8,128)(2,1)S(1)}, u32[]{:S(2)}, u32[]{:S(2)}) async-start(bf16[32,8,128]{2,1,0:T(8,128)(2,1)} %bitcast.4), calls=%async_computation.2 | async-start | bytes 131072 | tf_op jit(solution)/shard_map/all_to_all | solution.py:430
  57.3 1.0 %copy-start.6 = (f32[512,128]{1,0:T(8,128)S(1)}, f32[512,128]{1,0:T(8,128)}, u32[]{:S(2)}) copy-start(f32[512,128]{1,0:T(8,128)} %copy-done.5) | copy-start | bytes 786436
  58.3 0.8 %copy-start.8 = (s32[64,128]{1,0:T(8,128)S(1)}, s32[64,128]{1,0:T(8,128)}, u32[]{:S(2)}) copy-start(s32[64,128]{1,0:T(8,128)} %get-tuple-element.30.refs_4_) | copy-start | bytes 98308

commit v3 on v2

--- a/solution.py
+++ b/solution.py
@@ -145,23 +145,23 @@
     )(place, x, key_weight, value_weight)
 
 
-def pair_kernel(kept, taken, out):
+def pair_kernel(after, kept, taken, out):
     out[...] = (kept[...].astype(F32) + taken[...].astype(F32)).astype(BF16)
 
 
-def pair(kept, taken):
+def pair(after, kept, taken):
     return pl.pallas_call(
         pair_kernel,
         out_shape=jax.ShapeDtypeStruct(kept.shape, BF16),
-        in_specs=[VMEM] * 2,
+        in_specs=[ANY] + [VMEM] * 2,
         out_specs=VMEM,
         compiler_params=params(),
         name="pair",
-    )(kept, taken)
+    )(after, kept, taken)
 
 
 def cached_kernel(
-    lengths, after, q_in, cache_keys, cache_values, out, norms,
+    lengths, after, q_in, cache_keys, cache_values, out, norms, done,
     q, keys, values, q_rows, scores, weights, sems, *, scale
 ):
     moves = ((q_in, q), (cache_keys, keys), (cache_values, values))
@@ -199,6 +199,7 @@
     for r in range(requests):
         mine = pl.ds(r, rows, stride=requests)
         out[mine, :] = jnp.dot(weights[r], values[r, 0], preferred_element_type=F32)
+    done[...] = jnp.zeros_like(done)
 
 
 def cached_attention(lengths, after, q, cache_keys, cache_values):
@@ -207,9 +208,13 @@
     rows = steps * requests * (cols // head_dim)
     return pl.pallas_call(
         lambda *refs: cached_kernel(*refs, scale=1.0 / math.sqrt(head_dim)),
-        out_shape=(jax.ShapeDtypeStruct((rows, LANES), F32),) * 2,
+        out_shape=(
+            jax.ShapeDtypeStruct((rows, LANES), F32),
+            jax.ShapeDtypeStruct((rows, LANES), F32),
+            jax.ShapeDtypeStruct((8, LANES), F32),
+        ),
         in_specs=[SMEM, ANY] + [HBM] * 3,
-        out_specs=(VMEM,) * 2,
+        out_specs=(VMEM,) * 3,
         scratch_shapes=[pltpu.VMEM(a.shape, BF16) for a in (q, cache_keys, cache_values)]
         + [
             pltpu.VMEM((rows, head_dim), F32),
@@ -217,7 +222,7 @@
             pltpu.VMEM((requests, rows // requests, positions), BF16),
             pltpu.SemaphoreType.DMA((3,)),
         ],
-        compiler_params=params(),
+        compiler_params=params(60),
         cost_estimate=pl.CostEstimate(
             flops=4 * rows * positions * head_dim,
             bytes_accessed=4 * requests * positions * head_dim,
@@ -278,7 +283,7 @@
 
 
 def expand_kernel(
-    after, summands, ids, up, new_keys, keys_again, base_values, correction
+    summands, ids, up, new_keys, keys_again, base_values, correction
 ):
     sources, all_rows, lanes = summands.shape
     adapters, rank, head_dim = up.shape
@@ -306,7 +311,7 @@
     correction[...] = grown.astype(BF16)
 
 
-def expand(after, summands, ids, up):
+def expand(summands, ids, up):
     sources, all_rows, lanes = summands.shape
     rows = ids.shape[0]
     _, rank, head_dim = up.shape
@@ -319,11 +324,11 @@
             jax.ShapeDtypeStruct((tokens, head_dim), F32),
             jax.ShapeDtypeStruct((rows, head_dim), BF16),
         ),
-        in_specs=[ANY] + [VMEM] * 3,
+        in_specs=[VMEM] * 3,
         out_specs=(VMEM,) * 4,
         compiler_params=params(),
         name="expand",
-    )(after, summands, ids, up)
+    )(summands, ids, up)
 
 
 def weigh_kernel(q, new_keys, out, norms, slot_of_token, weights, mixed, chosen, *, scale):
@@ -437,10 +442,10 @@
     kept, given = project(place, normed_hidden_rows, key_weight, value_weight, tensor_size)
     neighbours = [(i, i ^ 1) for i in range(tensor_size)]
     taken = lax.ppermute(given, "tensor", neighbours)
-    summands, ids = shrink(received, adapter_down, pair(kept, taken))
-    cached = cached_attention(cache_lengths, summands, queries, cache_keys, cache_values)
+    *cached, done = cached_attention(cache_lengths, given, queries, cache_keys, cache_values)
+    summands, ids = shrink(received, adapter_down, pair(done, kept, taken))
     summands = exchange(summands, "tensor")
-    new_keys, fresh_keys, base_values, correction = expand(cached[0], summands, ids, adapter_up)
+    new_keys, fresh_keys, base_values, correction = expand(summands, ids, adapter_up)
     returned = exchange(correction, "batch")
     weights, mixed, chosen = weigh(
         queries, fresh_keys, *cached, slot_of_token, correction.shape[0]

time: 66.1 us -> 64.7 us (0.979)
  blocking collectives: 0 us -> 21.4 us
  waiting for transfers between devices: 22.3 us -> 9.01 us
  starting transfers between devices: 23.5 us -> 16.6 us
  local copies, waits for them, and re-layouts: 6.41 us -> 2.9 us
  Pallas kernels: 12.6 us -> 13.7 us
    all_to_all x0 -> x1, blocking collectives: none -> 21.4 us  [per_device(): lax.all_to_all(a, axis, split_axis=0, concat_axis=0, tiled=True)]
    all_to_all x3 -> x2, waiting for transfers between devices: 18.5 us -> 8.81 us  [per_device(): lax.all_to_all(a, axis, split_axis=0, concat_axis=0, tiled=True)]
    all_to_all x3 -> x2, starting transfers between devices: 21.8 us -> 14.9 us  [per_device(): lax.all_to_all(a, axis, split_axis=0, concat_axis=0, tiled=True)]
    ppermute x1, waiting for transfers between devices: 3.82 us -> 0.21 us  [per_device(): taken = lax.ppermute(given, 'tensor', neighbours)]
    unnamed x20 -> x16, local copies, waits for them, and re-layouts: 6.41 us -> 2.9 us
    pallas_call x1, Pallas kernels: 1.82 us -> 3.61 us  [cached_attention(): pl.pallas_call(lambda *refs: cached_kernel(*refs, scale=1.0 / math.sqrt(h...]
    pallas_call x1, Pallas kernels: 2.06 us -> 1.31 us  [shrink(): pl.pallas_call(shrink_kernel, out_shape=(jax.ShapeDtypeStruct((heads, tok...]
  transfers between devices with their start and end apart: 4 -> 3, of which waited for: 4 -> 3; matrix products, arithmetic and copies ran while one was open for 0% -> 0% of each run, Pallas kernels for 10% -> 13%
where the time goes in v3:
time: 64.7 us; the launch traced here: 64.4 us
  blocking collectives  21.4 us (33%)
  starting transfers between devices  16.6 us (26%)
  Pallas kernels  13.7 us (21%)
  waiting for transfers between devices  9.01 us (14%)
  local copies, waits for them, and re-layouts  2.9 us (4%)
  between operations  0.75 us (1%)
    all_to_all x1, blocking collectives, per_device(): lax.all_to_all(a, axis, split_axis=0, concat_axis=0, tiled=True)  21.4 us
    all_to_all x2, starting transfers between devices, per_device(): lax.all_to_all(a, axis, split_axis=0, concat_axis=0, tiled=True)  14.9 us
    all_to_all x2, waiting for transfers between devices, per_device(): lax.all_to_all(a, axis, split_axis=0, concat_axis=0, tiled=True)  8.81 us
    pallas_call x1, Pallas kernels, cached_attention(): pl.pallas_call(lambda *refs: cached_kernel(*refs, scale=1.0 / math.sqrt(h...  3.61 us
    pallas_call x1, Pallas kernels, project(): pl.pallas_call(project_kernel, out_shape=(jax.ShapeDtypeStruct((heads, to...  3.51 us
    unnamed x16, local copies, waits for them, and re-layouts  2.9 us
    pallas_call x1, Pallas kernels, pack(): pl.pallas_call(lambda *refs: pack_kernel(*refs, per_owner=per_owner), out...  2.11 us
    ppermute x1, starting transfers between devices, per_device(): taken = lax.ppermute(given, 'tensor', neighbours)  1.73 us
  transfers between devices with their start and end apart: 3, of which 3 were waited for; matrix products, arithmetic and copies ran while one was open for 0% of the time, Pallas kernels for 13%

profile of v3, /device:TPU:1, one launch (start us, length us, event | category | flops | bytes accessed | tf_op | source)
XLA Modules:
  0.0 64.4 jit_solution(10293135853626208634)
XLA Ops:
  0.6 2.1 %pack.1 = (bf16[256,1152]{1,0:T(8,128)(2,1)}, s32[64,128]{1,0:T(8,128)}) custom-call(s32[16]{0:T(128)} %refs_0_.3, s32[1024]{0:T(1024)} %refs_1_.1, bf16[4,16,1024]{2,1,0:T(8,128)(2,1)} %x_in.1), custom_call_target="tpu_custom_call" | custom-call | tf_op jit(solution)/shard_map/pack/pallas_call | solution.py:84
  2.8 8.6 %all-to-all-start = ((bf16[32,8,1152]{2,1,0:T(8,128)(2,1)}), bf16[32,8,1152]{2,1,0:T(8,128)(2,1)S(1)}, u32[]{:S(2)}, u32[]{:S(2)}) async-start(bf16[32,8,1152]{2,1,0:T(8,128)(2,1)} %bitcast.9), calls=%async_computation | async-start | bytes 1179648 | tf_op jit(solution)/shard_map/all_to_all | solution.py:435
  11.4 3.5 %project.1 = (bf16[8,64,128]{2,1,0:T(8,128)(2,1)}, bf16[8,64,128]{2,1,0:T(8,128)(2,1)}) custom-call(s32[1]{0:T(128)} %bitcast.2.place, bf16[4,16,1024]{2,1,0:T(8,128)(2,1)} %x_in.1, bf16[1024,1024]{1,0:T(8,128)(2,1)} %key_in.1, bf16[1024,1024]{1,0:T(8,128)(2,1)} %value_in.1), custom_call_target="tpu_custom_call" | custom-call | flops 268435456 | bytes 4194304 | tf_op jit(solution)/shard_map/project/pallas_call | solution.py:131
  14.9 0.0 copy-start.5
  14.9 1.7 %collective-permute-start = (bf16[8,64,128]{2,1,0:T(8,128)(2,1)}, bf16[8,64,128]{2,1,0:T(8,128)(2,1)S(1)}, u32[]{:S(2)}, u32[]{:S(2)}) collective-permute-start(bf16[8,64,128]{2,1,0:T(8,128)(2,1)} %get-tuple-element.22.refs_1_), channel_id=1, source_target_pairs={{0,1},{1,0},{2,3},{3,2},{4,5},{5,4},{6,7},{7,6},{8,9},{9,8},{10,11... | collective-permute-start | bytes 393224 | tf_op jit(solution)/shard_map/ppermute | solution.py:444
  16.6 3.6 %cached.1 = (f32[512,128]{1,0:T(8,128)}, f32[512,128]{1,0:T(8,128)}, f32[8,128]{1,0:T(8,128)}) custom-call(s32[16]{0:T(128)} %refs_0_.4, bf16[8,64,128]{2,1,0:T(8,128)(2,1)} %get-tuple-element.22.refs_1_, bf16[4,16,1024]{2,1,0:T(8,128)(2,1)} %refs_0_.5, bf16[16,1,256,128]{3,2,1,0:T(8,128)(2,1)} %refs_3_.1, bf16[16,1,256,128]{3,2,1,0:T(8,128)(2,1)} %refs_4_.1), custom_call_target="tpu_custom_call" | custom-call | flops 67108864 | bytes 2097152 | tf_op jit(solution)/shard_map/cached/pallas_call | solution.py:209
  20.2 0.2 collective-permute-done.taken
  20.4 0.0 copy-done.5
  20.4 0.0 copy-start.7
  20.4 0.7 %copy-done.7 = f32[8,128]{1,0:T(8,128)S(1)} copy-done((f32[8,128]{1,0:T(8,128)S(1)}, f32[8,128]{1,0:T(8,128)}, u32[]{:S(2)}) %copy-start.7) | copy-done | bytes 4120
  21.2 2.4 %all-to-all-done = bf16[32,8,1152]{2,1,0:T(8,128)(2,1)S(1)} async-done(((bf16[32,8,1152]{2,1,0:T(8,128)(2,1)}), bf16[32,8,1152]{2,1,0:T(8,128)(2,1)S(1)}, u32[]{:S(2)}, u32[]{:S(2)}) %all-to-all-start) | async-done | bytes 589856 | tf_op jit(solution)/shard_map/all_to_all | solution.py:435
  23.6 0.0 copy-start
  23.6 2.2 %copy-done = bf16[32,64,1024]{2,1,0:T(8,128)(2,1)S(1)} copy-done((bf16[32,64,1024]{2,1,0:T(8,128)(2,1)S(1)}, bf16[32,64,1024]{2,1,0:T(8,128)(2,1)}, u32[]{:S(2)}) %copy-start) | copy-done | bytes 4194328
  25.8 0.0 copy-start.2
  25.8 0.0 copy-start.1
  25.8 0.0 copy-start.3
  25.8 0.0 copy-start.4
  25.8 0.0 copy-start.6
  25.8 1.3 %shrink.1 = (bf16[8,192,128]{2,1,0:T(8,128)(2,1)S(1)}, bf16[256,128]{1,0:T(8,128)(2,1)S(1)}) custom-call(bf16[256,1152]{1,0:T(8,128)(2,1)S(1)} %bitcast.7, bf16[32,64,1024]{2,1,0:T(8,128)(2,1)S(1)} %copy-done, bf16[8,64,128]{2,1,0:T(8,128)(2,1)S(1)} %pair.1.partials), custom_call_target="tpu_custom_call" | custom-call | flops 1073741824 | bytes 4194304 | tf_op jit(solution)/shard_map/shrink/pallas_call | solution.py:263
  27.1 21.4 %all_to_all.27.summands = bf16[8,192,128]{2,1,0:T(8,128)(2,1)S(1)} all-to-all(bf16[8,192,128]{2,1,0:T(8,128)(2,1)S(1)} %get-tuple-element.25), channel_id=1, replica_groups=mesh['batch'=32,'tensor'=8] {'tensor'}, dimensions={0} | all-to-all | bytes 786432 | tf_op jit(solution)/shard_map/all_to_all | solution.py:435
  48.6 0.0 copy-done.2
  48.6 1.2 %expand.1 = (bf16[64,128]{1,0:T(8,128)(2,1)}, bf16[64,128]{1,0:T(8,128)(2,1)S(1)}, f32[64,128]{1,0:T(8,128)S(1)}, bf16[256,128]{1,0:T(8,128)(2,1)}) custom-call(bf16[8,192,128]{2,1,0:T(8,128)(2,1)S(1)} %all_to_all.27.summands, bf16[256,128]{1,0:T(8,128)(2,1)S(1)} %get-tuple-element.26.ids, bf16[32,64,128]{2,1,0:T(8,128)(2,1)S(1)} %copy-done.2), custom_call_target="tpu_custom_call" | custom-call | tf_op jit(solution)/shard_map/expand/pallas_call | solution.py:319
  49.8 6.3 %all-to-all-start.2 = ((bf16[32,8,128]{2,1,0:T(8,128)(2,1)}), bf16[32,8,128]{2,1,0:T(8,128)(2,1)S(1)}, u32[]{:S(2)}, u32[]{:S(2)}) async-start(bf16[32,8,128]{2,1,0:T(8,128)(2,1)} %bitcast.4), calls=%async_computation.2 | async-start | bytes 131072 | tf_op jit(solution)/shard_map/all_to_all | solution.py:435
  56.1 0.0 copy-done.1
  56.1 0.0 copy-done.3
  56.1 0.0 copy-done.4
  56.1 0.0 copy-done.6
  56.1 0.9 %weigh.1 = (bf16[512,64]{1,0:T(8,128)(2,1)S(1)}, f32[512,128]{1,0:T(8,128)S(1)}, bf16[64,256]{1,0:T(8,128)(2,1)S(1)}) custom-call(bf16[4,16,1024]{2,1,0:T(8,128)(2,1)S(1)} %copy-done.1, bf16[64,128]{1,0:T(8,128)(2,1)S(1)} %get-tuple-element.29.refs_1_, f32[512,128]{1,0:T(8,128)S(1)} %copy-done.3, f32[512,128]{1,0:T(8,128)S(1)} %copy-done.4, ...), custom_call_target="tpu_custom_call" | custom-call | flops 16777216 | bytes 1048576 | tf_op jit(solution)/shard_map/weigh/pallas_call | solution.py:368
  57.0 6.4 %all-to-all-done.2 = bf16[32,8,128]{2,1,0:T(8,128)(2,1)S(1)} async-done(((bf16[32,8,128]{2,1,0:T(8,128)(2,1)}), bf16[32,8,128]{2,1,0:T(8,128)(2,1)S(1)}, u32[]{:S(2)}, u32[]{:S(2)}) %all-to-all-start.2) | async-done | bytes 65568 | tf_op jit(solution)/shard_map/all_to_all | solution.py:435
  63.4 1.0 %finish.1 = (bf16[64,128]{1,0:T(8,128)(2,1)}, bf16[4,16,1024]{2,1,0:T(8,128)(2,1)}) custom-call(bf16[256,128]{1,0:T(8,128)(2,1)S(1)} %bitcast.8, bf16[64,256]{1,0:T(8,128)(2,1)S(1)} %get-tuple-element.33.chosen, f32[64,128]{1,0:T(8,128)S(1)} %get-tuple-element.34.base_values, bf16[512,64]{1,0:T(8,128)(2,1)S(1)} %get-tuple-element.35.weights, ...), custom_call_target="tpu_custom_call" | custom-call | tf_op jit(solution)/shard_map/finish/pallas_call | solution.py:406
  (1 shorter events, 0.0 us)
Async XLA Ops:
  2.8 20.9 %all-to-all-start = ((bf16[32,8,1152]{2,1,0:T(8,128)(2,1)}), bf16[32,8,1152]{2,1,0:T(8,128)(2,1)S(1)}, u32[]{:S(2)}, u32[]{:S(2)}) async-start(bf16[32,8,1152]{2,1,0:T(8,128)(2,1)} %bitcast.9), calls=%async_computation | async-start | bytes 1179648 | tf_op jit(solution)/shard_map/all_to_all | solution.py:435
  14.9 5.6 %copy-start.5 = (bf16[8,64,128]{2,1,0:T(8,128)(2,1)S(1)}, bf16[8,64,128]{2,1,0:T(8,128)(2,1)}, u32[]{:S(2)}) copy-start(bf16[8,64,128]{2,1,0:T(8,128)(2,1)} %get-tuple-element.24.kept) | copy-start | bytes 393220
  14.9 5.6 %collective-permute-start = (bf16[8,64,128]{2,1,0:T(8,128)(2,1)}, bf16[8,64,128]{2,1,0:T(8,128)(2,1)S(1)}, u32[]{:S(2)}, u32[]{:S(2)}) collective-permute-start(bf16[8,64,128]{2,1,0:T(8,128)(2,1)} %get-tuple-element.22.refs_1_), channel_id=1, source_target_pairs={{0,1},{1,0},{2,3},{3,2},{4,5},{5,4},{6,7},{7,6},{8,9},{9,8},{10,11... | collective-permute-start | bytes 393224 | tf_op jit(solution)/shard_map/ppermute | solution.py:444
  20.4 0.7 %copy-start.7 = (f32[8,128]{1,0:T(8,128)S(1)}, f32[8,128]{1,0:T(8,128)}, u32[]{:S(2)}) copy-start(f32[8,128]{1,0:T(8,128)} %get-tuple-element.23.after) | copy-start | bytes 12292
  23.6 2.2 %copy-start = (bf16[32,64,1024]{2,1,0:T(8,128)(2,1)S(1)}, bf16[32,64,1024]{2,1,0:T(8,128)(2,1)}, u32[]{:S(2)}) copy-start(bf16[32,64,1024]{2,1,0:T(8,128)(2,1)} %down.1) | copy-start | bytes 12582916
  25.8 22.8 %copy-start.2 = (bf16[32,64,128]{2,1,0:T(8,128)(2,1)S(1)}, bf16[32,64,128]{2,1,0:T(8,128)(2,1)}, u32[]{:S(2)}) copy-start(bf16[32,64,128]{2,1,0:T(8,128)(2,1)} %up.1) | copy-start | bytes 1572868
  25.8 30.3 %copy-start.1 = (bf16[4,16,1024]{2,1,0:T(8,128)(2,1)S(1)}, bf16[4,16,1024]{2,1,0:T(8,128)(2,1)}, u32[]{:S(2)}) copy-start(bf16[4,16,1024]{2,1,0:T(8,128)(2,1)} %refs_0_.5) | copy-start | bytes 393220
  25.8 30.3 %copy-start.3 = (f32[512,128]{1,0:T(8,128)S(1)}, f32[512,128]{1,0:T(8,128)}, u32[]{:S(2)}) copy-start(f32[512,128]{1,0:T(8,128)} %get-tuple-element.30.refs_2_) | copy-start | bytes 786436
  25.8 30.3 %copy-start.4 = (f32[512,128]{1,0:T(8,128)S(1)}, f32[512,128]{1,0:T(8,128)}, u32[]{:S(2)}) copy-start(f32[512,128]{1,0:T(8,128)} %get-tuple-element.31.refs_3_) | copy-start | bytes 786436
  25.8 30.3 %copy-start.6 = (s32[64,128]{1,0:T(8,128)S(1)}, s32[64,128]{1,0:T(8,128)}, u32[]{:S(2)}) copy-start(s32[64,128]{1,0:T(8,128)} %get-tuple-element.32.refs_4_) | copy-start | bytes 98308
  49.8 13.6 %all-to-all-start.2 = ((bf16[32,8,128]{2,1,0:T(8,128)(2,1)}), bf16[32,8,128]{2,1,0:T(8,128)(2,1)S(1)}, u32[]{:S(2)}, u32[]{:S(2)}) async-start(bf16[32,8,128]{2,1,0:T(8,128)(2,1)} %bitcast.4), calls=%async_computation.2 | async-start | bytes 131072 | tf_op jit(solution)/shard_map/all_to_all | solution.py:435

commit v4 on v2

--- a/solution.py
+++ b/solution.py
@@ -101,47 +101,53 @@
     )(adapter_ids, owner_map, x)
 
 
-def project_kernel(place, x_in, key_in, value_in, kept, given, x, key_weight, value_weight, sems):
-    moves = ((x_in, x), (key_in, key_weight), (value_in, value_weight))
-    copies = [
-        pltpu.make_async_copy(source, target, sems.at[i])
-        for i, (source, target) in enumerate(moves)
-    ]
-    for copy in copies:
-        copy.start()
-    heads, tokens, head_dim = kept.shape
-    copies[0].wait()
+def start_weight(wanted_keys, key_in, value_in, weight, sem):
+    @pl.when(wanted_keys)
+    def _():
+        pltpu.make_async_copy(key_in, weight, sem).start()
+
+    @pl.when(jnp.logical_not(wanted_keys))
+    def _():
+        pltpu.make_async_copy(value_in, weight, sem).start()
+
+    return pltpu.make_async_copy(key_in, weight, sem)
+
+
+def project(x, weight, out):
+    heads, tokens, head_dim = out.shape
     rows = x[...].reshape(tokens, x.shape[2])
-    copies[1].wait()
-    keys = jnp.dot(rows, key_weight[...], preferred_element_type=F32)
-    copies[2].wait()
-    values = jnp.dot(rows, value_weight[...], preferred_element_type=F32)
-    even = place[0] % 2 == 0
-    mine = jnp.where(even, keys, values).astype(BF16)
-    other = jnp.where(even, values, keys).astype(BF16)
+    product = jnp.dot(rows, weight[...], preferred_element_type=F32).astype(BF16)
     for h in range(heads):
-        kept[h] = mine[:, h * head_dim : (h + 1) * head_dim]
-        given[h] = other[:, h * head_dim : (h + 1) * head_dim]
-
-
-def project(place, x, key_weight, value_weight, heads):
+        out[h] = product[:, h * head_dim : (h + 1) * head_dim]
+
+
+def given_kernel(place, x_in, key_in, value_in, given, x, weight, sems):
+    tokens_copy = pltpu.make_async_copy(x_in, x, sems.at[0])
+    weight_copy = start_weight(place[0] % 2 == 1, key_in, value_in, weight, sems.at[1])
+    tokens_copy.start()
+    tokens_copy.wait()
+    weight_copy.wait()
+    project(x, weight, given)
+
+
+def given_sums(place, x, key_weight, value_weight, heads):
     steps, requests, cols = x.shape
     tokens = steps * requests
     head_dim = key_weight.shape[1] // heads
     return pl.pallas_call(
-        project_kernel,
-        out_shape=(jax.ShapeDtypeStruct((heads, tokens, head_dim), BF16),) * 2,
+        given_kernel,
+        out_shape=jax.ShapeDtypeStruct((heads, tokens, head_dim), BF16),
         in_specs=[SMEM] + [HBM] * 3,
-        out_specs=(VMEM,) * 2,
-        scratch_shapes=[pltpu.VMEM(a.shape, BF16) for a in (x, key_weight, value_weight)]
-        + [pltpu.SemaphoreType.DMA((3,))],
+        out_specs=VMEM,
+        scratch_shapes=[pltpu.VMEM(a.shape, BF16) for a in (x, key_weight)]
+        + [pltpu.SemaphoreType.DMA((2,))],
         compiler_params=params(60),
         cost_estimate=pl.CostEstimate(
-            flops=4 * tokens * cols * heads * head_dim,
-            bytes_accessed=4 * cols * heads * head_dim,
+            flops=2 * tokens * cols * heads * head_dim,
+            bytes_accessed=2 * cols * heads * head_dim,
             transcendentals=0,
         ),
-        name="project",
+        name="given",
     )(place, x, key_weight, value_weight)
 
 
@@ -161,16 +167,19 @@
 
 
 def cached_kernel(
-    lengths, after, q_in, cache_keys, cache_values, out, norms,
-    q, keys, values, q_rows, scores, weights, sems, *, scale
+    lengths, place, after, q_in, cache_keys, cache_values, x_in, key_in, value_in,
+    kept, out, norms,
+    q, keys, values, x, weight, q_rows, scores, weights, sems, *, scale
 ):
-    moves = ((q_in, q), (cache_keys, keys), (cache_values, values))
+    moves = ((q_in, q), (cache_keys, keys), (x_in, x), (cache_values, values))
     copies = [
         pltpu.make_async_copy(source, target, sems.at[i])
         for i, (source, target) in enumerate(moves)
     ]
-    for copy in copies:
+    for copy in copies[:3]:
         copy.start()
+    weight_copy = start_weight(place[0] % 2 == 0, key_in, value_in, weight, sems.at[4])
+    copies[3].start()
     steps, requests, cols = q.shape
     positions, head_dim = keys.shape[2], keys.shape[3]
     groups = cols // head_dim
@@ -196,35 +205,46 @@
         weights[r] = exponent.astype(BF16)
         norms[mine, :] = jnp.where(low, top, jnp.sum(exponent, axis=1, keepdims=True))
     copies[2].wait()
+    weight_copy.wait()
+    project(x, weight, kept)
+    copies[3].wait()
     for r in range(requests):
         mine = pl.ds(r, rows, stride=requests)
         out[mine, :] = jnp.dot(weights[r], values[r, 0], preferred_element_type=F32)
 
 
-def cached_attention(lengths, after, q, cache_keys, cache_values):
+def cached_attention(
+    lengths, place, after, q, cache_keys, cache_values, x, key_weight, value_weight
+):
     steps, requests, cols = q.shape
     positions, head_dim = cache_keys.shape[2], cache_keys.shape[3]
     rows = steps * requests * (cols // head_dim)
     return pl.pallas_call(
         lambda *refs: cached_kernel(*refs, scale=1.0 / math.sqrt(head_dim)),
-        out_shape=(jax.ShapeDtypeStruct((rows, LANES), F32),) * 2,
-        in_specs=[SMEM, ANY] + [HBM] * 3,
-        out_specs=(VMEM,) * 2,
-        scratch_shapes=[pltpu.VMEM(a.shape, BF16) for a in (q, cache_keys, cache_values)]
+        out_shape=(
+            jax.ShapeDtypeStruct(after.shape, BF16),
+            jax.ShapeDtypeStruct((rows, LANES), F32),
+            jax.ShapeDtypeStruct((rows, LANES), F32),
+        ),
+        in_specs=[SMEM, SMEM, ANY] + [HBM] * 6,
+        out_specs=(VMEM,) * 3,
+        scratch_shapes=[
+            pltpu.VMEM(a.shape, BF16) for a in (q, cache_keys, cache_values, x, key_weight)
+        ]
         + [
             pltpu.VMEM((rows, head_dim), F32),
             pltpu.VMEM((requests, rows // requests, positions), F32),
             pltpu.VMEM((requests, rows // requests, positions), BF16),
-            pltpu.SemaphoreType.DMA((3,)),
+            pltpu.SemaphoreType.DMA((5,)),
         ],
-        compiler_params=params(),
+        compiler_params=params(60),
         cost_estimate=pl.CostEstimate(
-            flops=4 * rows * positions * head_dim,
-            bytes_accessed=4 * requests * positions * head_dim,
+            flops=4 * rows * positions * head_dim + 2 * x.size * key_weight.shape[1],
+            bytes_accessed=4 * requests * positions * head_dim + 2 * key_weight.size,
             transcendentals=rows * positions,
         ),
         name="cached",
-    )(lengths, after, q, cache_keys, cache_values)
+    )(lengths, place, after, q, cache_keys, cache_values, x, key_weight, value_weight)
 
 
 def shrink_kernel(received, down, partials, out, ids):
@@ -278,7 +298,7 @@
 
 
 def expand_kernel(
-    after, summands, ids, up, new_keys, keys_again, base_values, correction
+    summands, ids, up, new_keys, keys_again, base_values, correction
 ):
     sources, all_rows, lanes = summands.shape
     adapters, rank, head_dim = up.shape
@@ -306,7 +326,7 @@
     correction[...] = grown.astype(BF16)
 
 
-def expand(after, summands, ids, up):
+def expand(summands, ids, up):
     sources, all_rows, lanes = summands.shape
     rows = ids.shape[0]
     _, rank, head_dim = up.shape
@@ -319,11 +339,11 @@
             jax.ShapeDtypeStruct((tokens, head_dim), F32),
             jax.ShapeDtypeStruct((rows, head_dim), BF16),
         ),
-        in_specs=[ANY] + [VMEM] * 3,
+        in_specs=[VMEM] * 3,
         out_specs=(VMEM,) * 4,
         compiler_params=params(),
         name="expand",
-    )(after, summands, ids, up)
+    )(summands, ids, up)
 
 
 def weigh_kernel(q, new_keys, out, norms, slot_of_token, weights, mixed, chosen, *, scale):
@@ -434,13 +454,23 @@
     )
     received = exchange(packed, "batch")
     place = lax.axis_index("tensor")[None]
-    kept, given = project(place, normed_hidden_rows, key_weight, value_weight, tensor_size)
+    given = given_sums(place, normed_hidden_rows, key_weight, value_weight, tensor_size)
     neighbours = [(i, i ^ 1) for i in range(tensor_size)]
     taken = lax.ppermute(given, "tensor", neighbours)
+    kept, *cached = cached_attention(
+        cache_lengths,
+        place,
+        given,
+        queries,
+        cache_keys,
+        cache_values,
+        normed_hidden_rows,
+        key_weight,
+        value_weight,
+    )
     summands, ids = shrink(received, adapter_down, pair(kept, taken))
-    cached = cached_attention(cache_lengths, summands, queries, cache_keys, cache_values)
     summands = exchange(summands, "tensor")
-    new_keys, fresh_keys, base_values, correction = expand(cached[0], summands, ids, adapter_up)
+    new_keys, fresh_keys, base_values, correction = expand(summands, ids, adapter_up)
     returned = exchange(correction, "batch")
     weights, mixed, chosen = weigh(
         queries, fresh_keys, *cached, slot_of_token, correction.shape[0]

time: 66.1 us -> 64.3 us (0.973)
  blocking collectives: 0 us -> 21.4 us
  waiting for transfers between devices: 22.3 us -> 8.9 us
  starting transfers between devices: 23.5 us -> 16.1 us
  local copies, waits for them, and re-layouts: 6.41 us -> 3.1 us
  Pallas kernels: 12.6 us -> 13.6 us
    all_to_all x0 -> x1, blocking collectives: none -> 21.4 us  [per_device(): lax.all_to_all(a, axis, split_axis=0, concat_axis=0, tiled=True)]
    all_to_all x3 -> x2, waiting for transfers between devices: 18.5 us -> 8.9 us  [per_device(): lax.all_to_all(a, axis, split_axis=0, concat_axis=0, tiled=True)]
    all_to_all x3 -> x2, starting transfers between devices: 21.8 us -> 14.4 us  [per_device(): lax.all_to_all(a, axis, split_axis=0, concat_axis=0, tiled=True)]
    ppermute x1, waiting for transfers between devices: 3.82 us -> 0.01 us  [per_device(): taken = lax.ppermute(given, 'tensor', neighbours)]
    unnamed x20 -> x14, local copies, waits for them, and re-layouts: 6.41 us -> 3.1 us
    pallas_call x1, Pallas kernels: 1.82 us -> 4.28 us  [cached_attention(): pl.pallas_call(lambda *refs: cached_kernel(*refs, scale=1.0 / math.sqrt(h...]
    pallas_call x1, Pallas kernels: 3.51 us -> 2.75 us  [given_sums(): pl.pallas_call(given_kernel, out_shape=jax.ShapeDtypeStruct((heads, token...]
    pallas_call x1, Pallas kernels: 2.06 us -> 1.32 us  [shrink(): pl.pallas_call(shrink_kernel, out_shape=(jax.ShapeDtypeStruct((heads, tok...]
  transfers between devices with their start and end apart: 4 -> 3, of which waited for: 4 -> 2; matrix products, arithmetic and copies ran while one was open for 0% -> 0% of each run, Pallas kernels for 10% -> 12%
where the time goes in v4:
time: 64.3 us; the launch traced here: 63.9 us
  blocking collectives  21.4 us (33%)
  starting transfers between devices  16.1 us (25%)
  Pallas kernels  13.6 us (21%)
  waiting for transfers between devices  8.9 us (14%)
  local copies, waits for them, and re-layouts  3.1 us (5%)
  between operations  0.75 us (1%)
    all_to_all x1, blocking collectives, per_device(): lax.all_to_all(a, axis, split_axis=0, concat_axis=0, tiled=True)  21.4 us
    all_to_all x2, starting transfers between devices, per_device(): lax.all_to_all(a, axis, split_axis=0, concat_axis=0, tiled=True)  14.4 us
    all_to_all x2, waiting for transfers between devices, per_device(): lax.all_to_all(a, axis, split_axis=0, concat_axis=0, tiled=True)  8.9 us
    pallas_call x1, Pallas kernels, cached_attention(): pl.pallas_call(lambda *refs: cached_kernel(*refs, scale=1.0 / math.sqrt(h...  4.28 us
    unnamed x14, local copies, waits for them, and re-layouts  3.1 us
    pallas_call x1, Pallas kernels, given_sums(): pl.pallas_call(given_kernel, out_shape=jax.ShapeDtypeStruct((heads, token...  2.75 us
    pallas_call x1, Pallas kernels, pack(): pl.pallas_call(lambda *refs: pack_kernel(*refs, per_owner=per_owner), out...  2.12 us
    ppermute x1, starting transfers between devices, per_device(): taken = lax.ppermute(given, 'tensor', neighbours)  1.73 us
  transfers between devices with their start and end apart: 3, of which 2 were waited for; matrix products, arithmetic and copies ran while one was open for 0% of the time, Pallas kernels for 12%

profile of v4, /device:TPU:1, one launch (start us, length us, event | category | flops | bytes accessed | tf_op | source)
XLA Modules:
  0.0 63.9 jit_solution(10524263716330655889)
XLA Ops:
  0.6 2.1 %pack.1 = (bf16[256,1152]{1,0:T(8,128)(2,1)}, s32[64,128]{1,0:T(8,128)}) custom-call(s32[16]{0:T(128)} %refs_0_.3, s32[1024]{0:T(1024)} %refs_1_.1, bf16[4,16,1024]{2,1,0:T(8,128)(2,1)} %refs_6_.1), custom_call_target="tpu_custom_call" | custom-call | tf_op jit(solution)/shard_map/pack/pallas_call | solution.py:84
  2.8 8.6 %all-to-all-start = ((bf16[32,8,1152]{2,1,0:T(8,128)(2,1)}), bf16[32,8,1152]{2,1,0:T(8,128)(2,1)S(1)}, u32[]{:S(2)}, u32[]{:S(2)}) async-start(bf16[32,8,1152]{2,1,0:T(8,128)(2,1)} %bitcast.9), calls=%async_computation | async-start | bytes 1179648 | tf_op jit(solution)/shard_map/all_to_all | solution.py:450
  11.4 2.8 %given.1.refs_2_ = bf16[8,64,128]{2,1,0:T(8,128)(2,1)} custom-call(s32[1]{0:T(128)} %bitcast.2.place.refs_1_, bf16[4,16,1024]{2,1,0:T(8,128)(2,1)} %refs_6_.1, bf16[1024,1024]{1,0:T(8,128)(2,1)} %refs_7_.1, bf16[1024,1024]{1,0:T(8,128)(2,1)} %refs_8_.1), custom_call_target="tpu_custom_call" | custom-call | flops 134217728 | bytes 2097152 | tf_op jit(solution)/shard_map/given/pallas_call | solution.py:137
  14.1 1.7 %collective-permute-start = (bf16[8,64,128]{2,1,0:T(8,128)(2,1)}, bf16[8,64,128]{2,1,0:T(8,128)(2,1)S(1)}, u32[]{:S(2)}, u32[]{:S(2)}) collective-permute-start(bf16[8,64,128]{2,1,0:T(8,128)(2,1)} %given.1.refs_2_), channel_id=1, source_target_pairs={{0,1},{1,0},{2,3},{3,2},{4,5},{5,4},{6,7},{7,6},{8,9},{9,8},{10,11... | collective-permute-start | bytes 393224 | tf_op jit(solution)/shard_map/ppermute | solution.py:459
  15.9 4.3 %cached.1 = (bf16[8,64,128]{2,1,0:T(8,128)(2,1)}, f32[512,128]{1,0:T(8,128)}, f32[512,128]{1,0:T(8,128)}) custom-call(s32[16]{0:T(128)} %refs_0_.4, s32[1]{0:T(128)} %bitcast.2.place.refs_1_, bf16[8,64,128]{2,1,0:T(8,128)(2,1)} %given.1.refs_2_, bf16[4,16,1024]{2,1,0:T(8,128)(2,1)} %refs_0_.5, bf16[16,1,256,128]{3,2,1,0:T(8,128)(2,1)} %refs_4_.1, ...), custom_call_target="tpu_custom_call" | custom-call | flops 201326592 | bytes 4194304 | tf_op jit(solution)/shard_map/cached/pallas_call | solution.py:222
  20.1 0.0 collective-permute-done.taken
  20.2 0.0 copy-start.5
  20.2 0.9 %copy-done.5 = bf16[8,64,128]{2,1,0:T(8,128)(2,1)S(1)} copy-done((bf16[8,64,128]{2,1,0:T(8,128)(2,1)S(1)}, bf16[8,64,128]{2,1,0:T(8,128)(2,1)}, u32[]{:S(2)}) %copy-start.5) | copy-done | bytes 131096
  21.1 2.5 %all-to-all-done = bf16[32,8,1152]{2,1,0:T(8,128)(2,1)S(1)} async-done(((bf16[32,8,1152]{2,1,0:T(8,128)(2,1)}), bf16[32,8,1152]{2,1,0:T(8,128)(2,1)S(1)}, u32[]{:S(2)}, u32[]{:S(2)}) %all-to-all-start) | async-done | bytes 589856 | tf_op jit(solution)/shard_map/all_to_all | solution.py:450
  23.6 0.0 copy-start
  23.6 2.2 %copy-done = bf16[32,64,1024]{2,1,0:T(8,128)(2,1)S(1)} copy-done((bf16[32,64,1024]{2,1,0:T(8,128)(2,1)S(1)}, bf16[32,64,1024]{2,1,0:T(8,128)(2,1)}, u32[]{:S(2)}) %copy-start) | copy-done | bytes 4194328
  25.8 0.0 copy-start.2
  25.8 0.0 copy-start.1
  25.8 0.0 copy-start.3
  25.8 0.0 copy-start.4
  25.8 0.0 copy-start.6
  25.8 1.3 %shrink.1 = (bf16[8,192,128]{2,1,0:T(8,128)(2,1)S(1)}, bf16[256,128]{1,0:T(8,128)(2,1)S(1)}) custom-call(bf16[256,1152]{1,0:T(8,128)(2,1)S(1)} %bitcast.7, bf16[32,64,1024]{2,1,0:T(8,128)(2,1)S(1)} %copy-done, bf16[8,64,128]{2,1,0:T(8,128)(2,1)S(1)} %pair.1.partials), custom_call_target="tpu_custom_call" | custom-call | flops 1073741824 | bytes 4194304 | tf_op jit(solution)/shard_map/shrink/pallas_call | solution.py:278
  27.1 21.4 %all_to_all.27.summands = bf16[8,192,128]{2,1,0:T(8,128)(2,1)S(1)} all-to-all(bf16[8,192,128]{2,1,0:T(8,128)(2,1)S(1)} %get-tuple-element.21), channel_id=1, replica_groups=mesh['batch'=32,'tensor'=8] {'tensor'}, dimensions={0} | all-to-all | bytes 786432 | tf_op jit(solution)/shard_map/all_to_all | solution.py:450
  48.6 0.0 copy-done.2
  48.6 1.2 %expand.1 = (bf16[64,128]{1,0:T(8,128)(2,1)}, bf16[64,128]{1,0:T(8,128)(2,1)S(1)}, f32[64,128]{1,0:T(8,128)S(1)}, bf16[256,128]{1,0:T(8,128)(2,1)}) custom-call(bf16[8,192,128]{2,1,0:T(8,128)(2,1)S(1)} %all_to_all.27.summands, bf16[256,128]{1,0:T(8,128)(2,1)S(1)} %get-tuple-element.22.ids, bf16[32,64,128]{2,1,0:T(8,128)(2,1)S(1)} %copy-done.2), custom_call_target="tpu_custom_call" | custom-call | tf_op jit(solution)/shard_map/expand/pallas_call | solution.py:334
  49.8 5.8 %all-to-all-start.2 = ((bf16[32,8,128]{2,1,0:T(8,128)(2,1)}), bf16[32,8,128]{2,1,0:T(8,128)(2,1)S(1)}, u32[]{:S(2)}, u32[]{:S(2)}) async-start(bf16[32,8,128]{2,1,0:T(8,128)(2,1)} %bitcast.4), calls=%async_computation.2 | async-start | bytes 131072 | tf_op jit(solution)/shard_map/all_to_all | solution.py:450
  55.6 0.0 copy-done.1
  55.6 0.0 copy-done.3
  55.6 0.0 copy-done.4
  55.6 0.0 copy-done.6
  55.6 0.9 %weigh.1 = (bf16[512,64]{1,0:T(8,128)(2,1)S(1)}, f32[512,128]{1,0:T(8,128)S(1)}, bf16[64,256]{1,0:T(8,128)(2,1)S(1)}) custom-call(bf16[4,16,1024]{2,1,0:T(8,128)(2,1)S(1)} %copy-done.1, bf16[64,128]{1,0:T(8,128)(2,1)S(1)} %get-tuple-element.25.refs_1_, f32[512,128]{1,0:T(8,128)S(1)} %copy-done.3, f32[512,128]{1,0:T(8,128)S(1)} %copy-done.4, ...), custom_call_target="tpu_custom_call" | custom-call | flops 16777216 | bytes 1048576 | tf_op jit(solution)/shard_map/weigh/pallas_call | solution.py:383
  56.6 6.4 %all-to-all-done.2 = bf16[32,8,128]{2,1,0:T(8,128)(2,1)S(1)} async-done(((bf16[32,8,128]{2,1,0:T(8,128)(2,1)}), bf16[32,8,128]{2,1,0:T(8,128)(2,1)S(1)}, u32[]{:S(2)}, u32[]{:S(2)}) %all-to-all-start.2) | async-done | bytes 65568 | tf_op jit(solution)/shard_map/all_to_all | solution.py:450
  62.9 1.0 %finish.1 = (bf16[64,128]{1,0:T(8,128)(2,1)}, bf16[4,16,1024]{2,1,0:T(8,128)(2,1)}) custom-call(bf16[256,128]{1,0:T(8,128)(2,1)S(1)} %bitcast.8, bf16[64,256]{1,0:T(8,128)(2,1)S(1)} %get-tuple-element.29.chosen, f32[64,128]{1,0:T(8,128)S(1)} %get-tuple-element.30.base_values, bf16[512,64]{1,0:T(8,128)(2,1)S(1)} %get-tuple-element.31.weights, ...), custom_call_target="tpu_custom_call" | custom-call | tf_op jit(solution)/shard_map/finish/pallas_call | solution.py:421
  (1 shorter events, 0.0 us)
Async XLA Ops:
  2.8 20.9 %all-to-all-start = ((bf16[32,8,1152]{2,1,0:T(8,128)(2,1)}), bf16[32,8,1152]{2,1,0:T(8,128)(2,1)S(1)}, u32[]{:S(2)}, u32[]{:S(2)}) async-start(bf16[32,8,1152]{2,1,0:T(8,128)(2,1)} %bitcast.9), calls=%async_computation | async-start | bytes 1179648 | tf_op jit(solution)/shard_map/all_to_all | solution.py:450
  14.1 6.0 %collective-permute-start = (bf16[8,64,128]{2,1,0:T(8,128)(2,1)}, bf16[8,64,128]{2,1,0:T(8,128)(2,1)S(1)}, u32[]{:S(2)}, u32[]{:S(2)}) collective-permute-start(bf16[8,64,128]{2,1,0:T(8,128)(2,1)} %given.1.refs_2_), channel_id=1, source_target_pairs={{0,1},{1,0},{2,3},{3,2},{4,5},{5,4},{6,7},{7,6},{8,9},{9,8},{10,11... | collective-permute-start | bytes 393224 | tf_op jit(solution)/shard_map/ppermute | solution.py:459
  20.2 0.9 %copy-start.5 = (bf16[8,64,128]{2,1,0:T(8,128)(2,1)S(1)}, bf16[8,64,128]{2,1,0:T(8,128)(2,1)}, u32[]{:S(2)}) copy-start(bf16[8,64,128]{2,1,0:T(8,128)(2,1)} %get-tuple-element.20.kept) | copy-start | bytes 393220
  23.6 2.2 %copy-start = (bf16[32,64,1024]{2,1,0:T(8,128)(2,1)S(1)}, bf16[32,64,1024]{2,1,0:T(8,128)(2,1)}, u32[]{:S(2)}) copy-start(bf16[32,64,1024]{2,1,0:T(8,128)(2,1)} %down.1) | copy-start | bytes 12582916
  25.8 22.8 %copy-start.2 = (bf16[32,64,128]{2,1,0:T(8,128)(2,1)S(1)}, bf16[32,64,128]{2,1,0:T(8,128)(2,1)}, u32[]{:S(2)}) copy-start(bf16[32,64,128]{2,1,0:T(8,128)(2,1)} %up.1) | copy-start | bytes 1572868
  25.8 29.8 %copy-start.1 = (bf16[4,16,1024]{2,1,0:T(8,128)(2,1)S(1)}, bf16[4,16,1024]{2,1,0:T(8,128)(2,1)}, u32[]{:S(2)}) copy-start(bf16[4,16,1024]{2,1,0:T(8,128)(2,1)} %refs_0_.5) | copy-start | bytes 393220
  25.8 29.8 %copy-start.3 = (f32[512,128]{1,0:T(8,128)S(1)}, f32[512,128]{1,0:T(8,128)}, u32[]{:S(2)}) copy-start(f32[512,128]{1,0:T(8,128)} %get-tuple-element.26.refs_2_) | copy-start | bytes 786436
  25.8 29.8 %copy-start.4 = (f32[512,128]{1,0:T(8,128)S(1)}, f32[512,128]{1,0:T(8,128)}, u32[]{:S(2)}) copy-start(f32[512,128]{1,0:T(8,128)} %get-tuple-element.27.refs_3_) | copy-start | bytes 786436
  25.8 29.8 %copy-start.6 = (s32[64,128]{1,0:T(8,128)S(1)}, s32[64,128]{1,0:T(8,128)}, u32[]{:S(2)}) copy-start(s32[64,128]{1,0:T(8,128)} %get-tuple-element.28.refs_4_) | copy-start | bytes 98308
  49.8 13.1 %all-to-all-start.2 = ((bf16[32,8,128]{2,1,0:T(8,128)(2,1)}), bf16[32,8,128]{2,1,0:T(8,128)(2,1)S(1)}, u32[]{:S(2)}, u32[]{:S(2)}) async-start(bf16[32,8,128]{2,1,0:T(8,128)(2,1)} %bitcast.4), calls=%async_computation.2 | async-start | bytes 131072 | tf_op jit(solution)/shard_map/all_to_all | solution.py:450

commit v5 on v4

--- a/solution.py
+++ b/solution.py
@@ -61,7 +61,7 @@
         owner = storage // per_owner
         rank = counts[owner]
         counts[owner] = rank + 1
-        slot = owner * CAP + rank
+        slot = (counts.shape[0] - 1 - owner) * CAP + rank
         slot_sub = jnp.where(token == r, slot, slot_sub)
         row_sub = jnp.where(token == r, storage - owner * per_owner, row_sub)
         slot_lane = jnp.where(column == r, slot, slot_lane)
@@ -247,7 +247,7 @@
     )(lengths, place, after, q, cache_keys, cache_values, x, key_weight, value_weight)
 
 
-def shrink_kernel(received, down, partials, out, ids):
+def shrink_kernel(received, down, partials, out, ids, *, order):
     adapters, rank, cols = down.shape
     rows = received.shape[0]
     per_part = 8
@@ -264,19 +264,19 @@
             partial = jnp.where(mine, products[i * rank : (i + 1) * rank], partial)
     partial = partial.astype(BF16)
     tokens = partials.shape[1]
-    for t in range(out.shape[0]):
-        out[t, :tokens] = partials[t]
+    for t, head in enumerate(order):
+        out[t, :tokens] = partials[head]
         for i in range(rows // LANES):
             start = tokens + i * rank
             out[t, start : start + rank] = partial[:, i * LANES : (i + 1) * LANES]
 
 
-def shrink(received, down, partials):
+def shrink(received, down, partials, order):
     adapters, rank, cols = down.shape
     rows = received.shape[0]
     heads, tokens, _ = partials.shape
     return pl.pallas_call(
-        shrink_kernel,
+        lambda *refs: shrink_kernel(*refs, order=order),
         out_shape=(
             jax.ShapeDtypeStruct((heads, tokens + rank * rows // LANES, LANES), BF16),
             jax.ShapeDtypeStruct((rows, LANES), BF16),
@@ -298,7 +298,7 @@
 
 
 def expand_kernel(
-    summands, ids, up, new_keys, keys_again, base_values, correction
+    summands, ids, up, new_keys, keys_again, base_values, correction, *, order
 ):
     sources, all_rows, lanes = summands.shape
     adapters, rank, head_dim = up.shape
@@ -306,10 +306,10 @@
     half = rows // 2
     tokens = all_rows - rank * rows // lanes
     add = lambda parts: sum((part.astype(F32) for part in parts[1:]), parts[0].astype(F32))
-    fresh = add([summands[t, :tokens] for t in range(0, sources, 2)]).astype(BF16)
+    fresh = add([summands[t, :tokens] for t in range(sources) if order[t] % 2 == 0]).astype(BF16)
     new_keys[...] = fresh
     keys_again[...] = fresh
-    base_values[...] = add([summands[t, :tokens] for t in range(1, sources, 2)])
+    base_values[...] = add([summands[t, :tokens] for t in range(sources) if order[t] % 2 == 1])
     packed = add([summands[t, tokens:] for t in range(sources)]).T
     turned = pltpu.roll(packed, rank, 1)
     low = iota((half, LANES), 1) < rank
@@ -326,13 +326,13 @@
     correction[...] = grown.astype(BF16)
 
 
-def expand(summands, ids, up):
+def expand(summands, ids, up, order):
     sources, all_rows, lanes = summands.shape
     rows = ids.shape[0]
     _, rank, head_dim = up.shape
     tokens = all_rows - rank * rows // lanes
     return pl.pallas_call(
-        expand_kernel,
+        lambda *refs: expand_kernel(*refs, order=order),
         out_shape=(
             jax.ShapeDtypeStruct((tokens, head_dim), BF16),
             jax.ShapeDtypeStruct((tokens, head_dim), BF16),
@@ -447,12 +447,16 @@
     steps, requests, _ = normed_hidden_rows.shape
     owners = lax.axis_size("batch")
     tensor_size = lax.axis_size("tensor")
-    exchange = lambda a, axis: lax.all_to_all(a, axis, split_axis=0, concat_axis=0, tiled=True)
+    owner_order = list(range(owners))[::-1]
+    tensor_order = list(range(tensor_size))[::-1]
+    exchange = lambda a, axis, order: lax.all_to_all(
+        a, axis, split_axis=0, concat_axis=0, axis_index_groups=[order], tiled=True
+    )
 
     packed, slot_of_token = pack(
         adapter_ids, owner_map, normed_hidden_rows, adapter_down.shape[0], owners
     )
-    received = exchange(packed, "batch")
+    received = exchange(packed, "batch", owner_order)
     place = lax.axis_index("tensor")[None]
     given = given_sums(place, normed_hidden_rows, key_weight, value_weight, tensor_size)
     neighbours = [(i, i ^ 1) for i in range(tensor_size)]
@@ -468,10 +472,10 @@
         key_weight,
         value_weight,
     )
-    summands, ids = shrink(received, adapter_down, pair(kept, taken))
-    summands = exchange(summands, "tensor")
-    new_keys, fresh_keys, base_values, correction = expand(summands, ids, adapter_up)
-    returned = exchange(correction, "batch")
+    summands, ids = shrink(received, adapter_down, pair(kept, taken), tensor_order)
+    summands = exchange(summands, "tensor", tensor_order)
+    new_keys, fresh_keys, base_values, correction = expand(summands, ids, adapter_up, tensor_order)
+    returned = exchange(correction, "batch", owner_order)
     weights, mixed, chosen = weigh(
         queries, fresh_keys, *cached, slot_of_token, correction.shape[0]
     )

time: 64.3 us -> 57.8 us (0.90)
  waiting for transfers between devices: 8.9 us -> 2.79 us
  blocking collectives: 21.4 us -> 15.9 us
  starting transfers between devices: 16.1 us -> 21.2 us
    all_to_all x2, waiting for transfers between devices: 8.9 us -> 2.79 us  [per_device(): lax.all_to_all(a, axis, split_axis=0, concat_axis=0, axis_index_groups=[o...]
    all_to_all x1, blocking collectives: 21.4 us -> 15.9 us  [per_device(): lax.all_to_all(a, axis, split_axis=0, concat_axis=0, axis_index_groups=[o...]
    all_to_all x2, starting transfers between devices: 14.4 us -> 19.5 us  [per_device(): lax.all_to_all(a, axis, split_axis=0, concat_axis=0, axis_index_groups=[o...]
  transfers between devices with their start and end apart: 3 -> 3, of which waited for: 2 -> 1; matrix products, arithmetic and copies ran while one was open for 0% -> 0% of each run, Pallas kernels for 12% -> 14%
where the time goes in v5:
time: 57.8 us; the launch traced here: 57.4 us
  starting transfers between devices  21.2 us (37%)
  blocking collectives  15.9 us (28%)
  Pallas kernels  13.6 us (24%)
  local copies, waits for them, and re-layouts  3.1 us (5%)
  waiting for transfers between devices  2.79 us (5%)
  between operations  0.77 us (1%)
    all_to_all x2, starting transfers between devices, per_device(): lax.all_to_all(a, axis, split_axis=0, concat_axis=0, axis_index_groups=[o...  19.5 us
    all_to_all x1, blocking collectives, per_device(): lax.all_to_all(a, axis, split_axis=0, concat_axis=0, axis_index_groups=[o...  15.9 us
    pallas_call x1, Pallas kernels, cached_attention(): pl.pallas_call(lambda *refs: cached_kernel(*refs, scale=1.0 / math.sqrt(h...  4.28 us
    unnamed x14, local copies, waits for them, and re-layouts  3.1 us
    all_to_all x2, waiting for transfers between devices, per_device(): lax.all_to_all(a, axis, split_axis=0, concat_axis=0, axis_index_groups=[o...  2.79 us
    pallas_call x1, Pallas kernels, given_sums(): pl.pallas_call(given_kernel, out_shape=jax.ShapeDtypeStruct((heads, token...  2.75 us
    pallas_call x1, Pallas kernels, pack(): pl.pallas_call(lambda *refs: pack_kernel(*refs, per_owner=per_owner), out...  2.13 us
    ppermute x1, starting transfers between devices, per_device(): taken = lax.ppermute(given, 'tensor', neighbours)  1.72 us
  transfers between devices with their start and end apart: 3, of which 1 were waited for; matrix products, arithmetic and copies ran while one was open for 0% of the time, Pallas kernels for 14%

profile of v5, /device:TPU:1, one launch (start us, length us, event | category | flops | bytes accessed | tf_op | source)
XLA Modules:
  0.0 57.4 jit_solution(4175054478914853868)
XLA Ops:
  0.6 2.1 %pack.1 = (bf16[256,1152]{1,0:T(8,128)(2,1)}, s32[64,128]{1,0:T(8,128)}) custom-call(s32[16]{0:T(128)} %refs_0_.3, s32[1024]{0:T(1024)} %refs_1_.2, bf16[4,16,1024]{2,1,0:T(8,128)(2,1)} %refs_6_.1), custom_call_target="tpu_custom_call" | custom-call | tf_op jit(solution)/shard_map/pack/pallas_call | solution.py:84
  2.8 9.6 %all-to-all-start = ((bf16[32,8,1152]{2,1,0:T(8,128)(2,1)}), bf16[32,8,1152]{2,1,0:T(8,128)(2,1)S(1)}, u32[]{:S(2)}, u32[]{:S(2)}) async-start(bf16[32,8,1152]{2,1,0:T(8,128)(2,1)} %bitcast.9), calls=%async_computation | async-start | bytes 1179648 | tf_op jit(solution)/shard_map/all_to_all | solution.py:452
  12.4 2.8 %given.1.refs_2_ = bf16[8,64,128]{2,1,0:T(8,128)(2,1)} custom-call(s32[1]{0:T(128)} %bitcast.2.place.refs_1_, bf16[4,16,1024]{2,1,0:T(8,128)(2,1)} %refs_6_.1, bf16[1024,1024]{1,0:T(8,128)(2,1)} %refs_7_.1, bf16[1024,1024]{1,0:T(8,128)(2,1)} %refs_8_.1), custom_call_target="tpu_custom_call" | custom-call | flops 134217728 | bytes 2097152 | tf_op jit(solution)/shard_map/given/pallas_call | solution.py:137
  15.2 1.7 %collective-permute-start = (bf16[8,64,128]{2,1,0:T(8,128)(2,1)}, bf16[8,64,128]{2,1,0:T(8,128)(2,1)S(1)}, u32[]{:S(2)}, u32[]{:S(2)}) collective-permute-start(bf16[8,64,128]{2,1,0:T(8,128)(2,1)} %given.1.refs_2_), channel_id=1, source_target_pairs={{0,1},{1,0},{2,3},{3,2},{4,5},{5,4},{6,7},{7,6},{8,9},{9,8},{10,11... | collective-permute-start | bytes 393224 | tf_op jit(solution)/shard_map/ppermute | solution.py:463
  16.9 4.3 %cached.1 = (bf16[8,64,128]{2,1,0:T(8,128)(2,1)}, f32[512,128]{1,0:T(8,128)}, f32[512,128]{1,0:T(8,128)}) custom-call(s32[16]{0:T(128)} %refs_0_.4, s32[1]{0:T(128)} %bitcast.2.place.refs_1_, bf16[8,64,128]{2,1,0:T(8,128)(2,1)} %given.1.refs_2_, bf16[4,16,1024]{2,1,0:T(8,128)(2,1)} %refs_0_.5, bf16[16,1,256,128]{3,2,1,0:T(8,128)(2,1)} %refs_4_.1, ...), custom_call_target="tpu_custom_call" | custom-call | flops 201326592 | bytes 4194304 | tf_op jit(solution)/shard_map/cached/pallas_call | solution.py:222
  21.2 0.0 collective-permute-done.taken
  21.2 0.0 copy-start.5
  21.2 0.9 %copy-done.5 = bf16[8,64,128]{2,1,0:T(8,128)(2,1)S(1)} copy-done((bf16[8,64,128]{2,1,0:T(8,128)(2,1)S(1)}, bf16[8,64,128]{2,1,0:T(8,128)(2,1)}, u32[]{:S(2)}) %copy-start.5) | copy-done | bytes 131096
  22.1 0.0 all-to-all-done
  22.1 0.0 copy-start
  22.2 2.2 %copy-done = bf16[32,64,1024]{2,1,0:T(8,128)(2,1)S(1)} copy-done((bf16[32,64,1024]{2,1,0:T(8,128)(2,1)S(1)}, bf16[32,64,1024]{2,1,0:T(8,128)(2,1)}, u32[]{:S(2)}) %copy-start) | copy-done | bytes 4194328
  24.3 0.0 copy-start.2
  24.3 0.0 copy-start.1
  24.3 0.0 copy-start.3
  24.3 0.0 copy-start.4
  24.4 0.0 copy-start.6
  24.4 1.3 %shrink.1 = (bf16[8,192,128]{2,1,0:T(8,128)(2,1)S(1)}, bf16[256,128]{1,0:T(8,128)(2,1)S(1)}) custom-call(bf16[256,1152]{1,0:T(8,128)(2,1)S(1)} %bitcast.7, bf16[32,64,1024]{2,1,0:T(8,128)(2,1)S(1)} %copy-done, bf16[8,64,128]{2,1,0:T(8,128)(2,1)S(1)} %pair.1.refs_2_), custom_call_target="tpu_custom_call" | custom-call | flops 1073741824 | bytes 4194304 | tf_op jit(solution)/shard_map/shrink/pallas_call | solution.py:278
  25.7 15.9 %all_to_all.27.refs_0_ = bf16[8,192,128]{2,1,0:T(8,128)(2,1)S(1)} all-to-all(bf16[8,192,128]{2,1,0:T(8,128)(2,1)S(1)} %get-tuple-element.21), channel_id=1, replica_groups={{7,6,5,4,3,2,1,0},{15,14,13,12,11,10,9,8},{23,22,21,20,19,18,17,16},{31..., dimensions={0} | all-to-all | bytes 786432 | tf_op jit(solution)/shard_map/all_to_all | solution.py:452
  41.6 0.0 copy-done.2
  41.6 1.2 %expand.1 = (bf16[64,128]{1,0:T(8,128)(2,1)}, bf16[64,128]{1,0:T(8,128)(2,1)S(1)}, f32[64,128]{1,0:T(8,128)S(1)}, bf16[256,128]{1,0:T(8,128)(2,1)}) custom-call(bf16[8,192,128]{2,1,0:T(8,128)(2,1)S(1)} %all_to_all.27.refs_0_, bf16[256,128]{1,0:T(8,128)(2,1)S(1)} %get-tuple-element.22.refs_1_, bf16[32,64,128]{2,1,0:T(8,128)(2,1)S(1)} %copy-done.2), custom_call_target="tpu_custom_call" | custom-call | tf_op jit(solution)/shard_map/expand/pallas_call | solution.py:334
  42.8 9.9 %all-to-all-start.2 = ((bf16[32,8,128]{2,1,0:T(8,128)(2,1)}), bf16[32,8,128]{2,1,0:T(8,128)(2,1)S(1)}, u32[]{:S(2)}, u32[]{:S(2)}) async-start(bf16[32,8,128]{2,1,0:T(8,128)(2,1)} %bitcast.4), calls=%async_computation.2 | async-start | bytes 131072 | tf_op jit(solution)/shard_map/all_to_all | solution.py:452
  52.7 0.0 copy-done.1
  52.7 0.0 copy-done.3
  52.7 0.0 copy-done.4
  52.7 0.0 copy-done.6
  52.7 0.9 %weigh.1 = (bf16[512,64]{1,0:T(8,128)(2,1)S(1)}, f32[512,128]{1,0:T(8,128)S(1)}, bf16[64,256]{1,0:T(8,128)(2,1)S(1)}) custom-call(bf16[4,16,1024]{2,1,0:T(8,128)(2,1)S(1)} %copy-done.1, bf16[64,128]{1,0:T(8,128)(2,1)S(1)} %get-tuple-element.25.refs_1_, f32[512,128]{1,0:T(8,128)S(1)} %copy-done.3, f32[512,128]{1,0:T(8,128)S(1)} %copy-done.4, ...), custom_call_target="tpu_custom_call" | custom-call | flops 16777216 | bytes 1048576 | tf_op jit(solution)/shard_map/weigh/pallas_call | solution.py:383
  53.7 2.8 %all-to-all-done.2 = bf16[32,8,128]{2,1,0:T(8,128)(2,1)S(1)} async-done(((bf16[32,8,128]{2,1,0:T(8,128)(2,1)}), bf16[32,8,128]{2,1,0:T(8,128)(2,1)S(1)}, u32[]{:S(2)}, u32[]{:S(2)}) %all-to-all-start.2) | async-done | bytes 65568 | tf_op jit(solution)/shard_map/all_to_all | solution.py:452
  56.4 1.0 %finish.1 = (bf16[64,128]{1,0:T(8,128)(2,1)}, bf16[4,16,1024]{2,1,0:T(8,128)(2,1)}) custom-call(bf16[256,128]{1,0:T(8,128)(2,1)S(1)} %bitcast.8, bf16[64,256]{1,0:T(8,128)(2,1)S(1)} %get-tuple-element.29.chosen, f32[64,128]{1,0:T(8,128)S(1)} %get-tuple-element.30.base_values, bf16[512,64]{1,0:T(8,128)(2,1)S(1)} %get-tuple-element.31.weights, ...), custom_call_target="tpu_custom_call" | custom-call | tf_op jit(solution)/shard_map/finish/pallas_call | solution.py:421
  (1 shorter events, 0.0 us)
Async XLA Ops:
  2.8 19.4 %all-to-all-start = ((bf16[32,8,1152]{2,1,0:T(8,128)(2,1)}), bf16[32,8,1152]{2,1,0:T(8,128)(2,1)S(1)}, u32[]{:S(2)}, u32[]{:S(2)}) async-start(bf16[32,8,1152]{2,1,0:T(8,128)(2,1)} %bitcast.9), calls=%async_computation | async-start | bytes 1179648 | tf_op jit(solution)/shard_map/all_to_all | solution.py:452
  15.2 6.0 %collective-permute-start = (bf16[8,64,128]{2,1,0:T(8,128)(2,1)}, bf16[8,64,128]{2,1,0:T(8,128)(2,1)S(1)}, u32[]{:S(2)}, u32[]{:S(2)}) collective-permute-start(bf16[8,64,128]{2,1,0:T(8,128)(2,1)} %given.1.refs_2_), channel_id=1, source_target_pairs={{0,1},{1,0},{2,3},{3,2},{4,5},{5,4},{6,7},{7,6},{8,9},{9,8},{10,11... | collective-permute-start | bytes 393224 | tf_op jit(solution)/shard_map/ppermute | solution.py:463
  21.2 0.9 %copy-start.5 = (bf16[8,64,128]{2,1,0:T(8,128)(2,1)S(1)}, bf16[8,64,128]{2,1,0:T(8,128)(2,1)}, u32[]{:S(2)}) copy-start(bf16[8,64,128]{2,1,0:T(8,128)(2,1)} %get-tuple-element.20.kept) | copy-start | bytes 393220
  22.1 2.2 %copy-start = (bf16[32,64,1024]{2,1,0:T(8,128)(2,1)S(1)}, bf16[32,64,1024]{2,1,0:T(8,128)(2,1)}, u32[]{:S(2)}) copy-start(bf16[32,64,1024]{2,1,0:T(8,128)(2,1)} %refs_1_.3) | copy-start | bytes 12582916
  24.3 17.3 %copy-start.2 = (bf16[32,64,128]{2,1,0:T(8,128)(2,1)S(1)}, bf16[32,64,128]{2,1,0:T(8,128)(2,1)}, u32[]{:S(2)}) copy-start(bf16[32,64,128]{2,1,0:T(8,128)(2,1)} %refs_2_.3) | copy-start | bytes 1572868
  24.3 28.4 %copy-start.1 = (bf16[4,16,1024]{2,1,0:T(8,128)(2,1)S(1)}, bf16[4,16,1024]{2,1,0:T(8,128)(2,1)}, u32[]{:S(2)}) copy-start(bf16[4,16,1024]{2,1,0:T(8,128)(2,1)} %refs_0_.5) | copy-start | bytes 393220
  24.3 28.4 %copy-start.3 = (f32[512,128]{1,0:T(8,128)S(1)}, f32[512,128]{1,0:T(8,128)}, u32[]{:S(2)}) copy-start(f32[512,128]{1,0:T(8,128)} %get-tuple-element.26.refs_2_) | copy-start | bytes 786436
  24.3 28.4 %copy-start.4 = (f32[512,128]{1,0:T(8,128)S(1)}, f32[512,128]{1,0:T(8,128)}, u32[]{:S(2)}) copy-start(f32[512,128]{1,0:T(8,128)} %get-tuple-element.27.refs_3_) | copy-start | bytes 786436
  24.4 28.4 %copy-start.6 = (s32[64,128]{1,0:T(8,128)S(1)}, s32[64,128]{1,0:T(8,128)}, u32[]{:S(2)}) copy-start(s32[64,128]{1,0:T(8,128)} %get-tuple-element.28.refs_4_) | copy-start | bytes 98308
  42.8 13.6 %all-to-all-start.2 = ((bf16[32,8,128]{2,1,0:T(8,128)(2,1)}), bf16[32,8,128]{2,1,0:T(8,128)(2,1)S(1)}, u32[]{:S(2)}, u32[]{:S(2)}) async-start(bf16[32,8,128]{2,1,0:T(8,128)(2,1)} %bitcast.4), calls=%async_computation.2 | async-start | bytes 131072 | tf_op jit(solution)/shard_map/all_to_all | solution.py:452

commit v6 on v5

--- a/solution.py
+++ b/solution.py
@@ -237,7 +237,7 @@
             pltpu.VMEM((requests, rows // requests, positions), BF16),
             pltpu.SemaphoreType.DMA((5,)),
         ],
-        compiler_params=params(60),
+        compiler_params=params(52),
         cost_estimate=pl.CostEstimate(
             flops=4 * rows * positions * head_dim + 2 * x.size * key_weight.shape[1],
             bytes_accessed=4 * requests * positions * head_dim + 2 * key_weight.size,
@@ -346,7 +346,9 @@
     )(summands, ids, up)
 
 
-def weigh_kernel(q, new_keys, out, norms, slot_of_token, weights, mixed, chosen, *, scale):
+def weigh_kernel(
+    q, new_keys, base_values, out, norms, slot_of_token, spread, mixed, chosen, *, scale
+):
     steps, requests, cols = q.shape
     tokens, head_dim = new_keys.shape
     slot_rows = chosen.shape[1]
@@ -356,6 +358,7 @@
     chosen[...] = jnp.where(found, 1.0, 0.0).astype(BF16)
     groups = cols // head_dim
     keys = new_keys[...]
+    base = base_values[...].astype(BF16)
     rows = groups * requests
     for s in range(steps):
         q_rows = jnp.concatenate(
@@ -372,22 +375,27 @@
         fresh = jnp.exp(scores - top)
         rescale = jnp.exp(cached_top - top)
         norm = 1.0 / (cached_sum * rescale + jnp.sum(fresh, axis=1, keepdims=True))
-        weights[part, :] = (fresh * norm).astype(BF16)
-        mixed[part, :] = out[part, :] * (rescale * norm)
-
-
-def weigh(q, new_keys, out, norms, slot_of_token, slot_rows):
+        weights = (fresh * norm).astype(BF16)
+        spread[part, :] = (
+            ADAPTER_SCALE * jnp.dot(weights, chosen[...], preferred_element_type=F32)
+        ).astype(BF16)
+        mixed[part, :] = out[part, :] * (rescale * norm) + jnp.dot(
+            weights, base, preferred_element_type=F32
+        )
+
+
+def weigh(q, new_keys, base_values, out, norms, slot_of_token, slot_rows):
     rows, head_dim = out.shape
     tokens = new_keys.shape[0]
     kernel = lambda *refs: weigh_kernel(*refs, scale=1.0 / math.sqrt(head_dim))
     return pl.pallas_call(
         kernel,
         out_shape=(
-            jax.ShapeDtypeStruct((rows, tokens), BF16),
+            jax.ShapeDtypeStruct((rows, slot_rows), BF16),
             jax.ShapeDtypeStruct((rows, head_dim), F32),
             jax.ShapeDtypeStruct((tokens, slot_rows), BF16),
         ),
-        in_specs=[VMEM] * 5,
+        in_specs=[VMEM] * 6,
         out_specs=(VMEM,) * 3,
         compiler_params=params(),
         cost_estimate=pl.CostEstimate(
@@ -396,20 +404,19 @@
             transcendentals=rows * tokens,
         ),
         name="weigh",
-    )(q, new_keys, out, norms, slot_of_token)
-
-
-def finish_kernel(returned, chosen, base_values, weights, mixed, values_out, attention):
+    )(q, new_keys, base_values, out, norms, slot_of_token)
+
+
+def finish_kernel(returned, chosen, base_values, spread, mixed, values_out, attention):
     steps, requests, cols = attention.shape
     tokens, head_dim = base_values.shape
     groups = cols // head_dim
     correction = jnp.dot(chosen[...], returned[...], preferred_element_type=F32)
-    values = (base_values[...] + ADAPTER_SCALE * correction).astype(BF16)
-    values_out[...] = values
+    values_out[...] = (base_values[...] + ADAPTER_SCALE * correction).astype(BF16)
     rows = groups * requests
     for s in range(steps):
         part = slice(s * rows, (s + 1) * rows)
-        fresh = jnp.dot(weights[part, :], values, preferred_element_type=F32)
+        fresh = jnp.dot(spread[part, :], returned[...], preferred_element_type=F32)
         result = (mixed[part, :] + fresh).astype(BF16)
         for g in range(groups):
             attention[s, :, g * head_dim : (g + 1) * head_dim] = result[
@@ -417,7 +424,7 @@
             ]
 
 
-def finish(returned, chosen, base_values, weights, mixed, attention_shape):
+def finish(returned, chosen, base_values, spread, mixed, attention_shape):
     return pl.pallas_call(
         finish_kernel,
         out_shape=(
@@ -428,7 +435,7 @@
         out_specs=(VMEM,) * 2,
         compiler_params=params(),
         name="finish",
-    )(returned, chosen, base_values, weights, mixed)
+    )(returned, chosen, base_values, spread, mixed)
 
 
 def per_device(
@@ -476,10 +483,10 @@
     summands = exchange(summands, "tensor", tensor_order)
     new_keys, fresh_keys, base_values, correction = expand(summands, ids, adapter_up, tensor_order)
     returned = exchange(correction, "batch", owner_order)
-    weights, mixed, chosen = weigh(
-        queries, fresh_keys, *cached, slot_of_token, correction.shape[0]
-    )
-    values, attention = finish(returned, chosen, base_values, weights, mixed, queries.shape)
+    spread, mixed, chosen = weigh(
+        queries, fresh_keys, base_values, *cached, slot_of_token, correction.shape[0]
+    )
+    values, attention = finish(returned, chosen, base_values, spread, mixed, queries.shape)
     shape = (steps, requests, new_keys.shape[1])
     return (new_keys.reshape(shape), values.reshape(shape), attention)
 

time: 57.8 us -> 57.5 us (level)
  waiting for transfers between devices: 2.79 us -> 1.6 us
  blocking collectives: 15.9 us -> 16.7 us
    pallas_call x1, Pallas kernels: 0.91 us -> 2.14 us  [weigh(): pl.pallas_call(kernel, out_shape=(jax.ShapeDtypeStruct((rows, slot_rows),...]
    all_to_all x2, waiting for transfers between devices: 2.79 us -> 1.59 us  [per_device(): lax.all_to_all(a, axis, split_axis=0, concat_axis=0, axis_index_groups=[o...]
    pallas_call x1, Pallas kernels: 4.28 us -> 3.48 us  [cached_attention(): pl.pallas_call(lambda *refs: cached_kernel(*refs, scale=1.0 / math.sqrt(h...]
    all_to_all x1, blocking collectives: 15.9 us -> 16.7 us  [per_device(): lax.all_to_all(a, axis, split_axis=0, concat_axis=0, axis_index_groups=[o...]
  transfers between devices with their start and end apart: 3 -> 3, of which waited for: 1 -> 1; matrix products, arithmetic and copies ran while one was open for 0% -> 0% of each run, Pallas kernels for 14% -> 15%
where the time goes in v6:
time: 57.5 us; the launch traced here: 57.2 us
  starting transfers between devices  21 us (37%)
  blocking collectives  16.7 us (29%)
  Pallas kernels  14 us (24%)
  local copies, waits for them, and re-layouts  3.13 us (5%)
  waiting for transfers between devices  1.6 us (3%)
  between operations  0.76 us (1%)
    all_to_all x2, starting transfers between devices, per_device(): lax.all_to_all(a, axis, split_axis=0, concat_axis=0, axis_index_groups=[o...  19.3 us
    all_to_all x1, blocking collectives, per_device(): lax.all_to_all(a, axis, split_axis=0, concat_axis=0, axis_index_groups=[o...  16.7 us
    pallas_call x1, Pallas kernels, cached_attention(): pl.pallas_call(lambda *refs: cached_kernel(*refs, scale=1.0 / math.sqrt(h...  3.48 us
    unnamed x14, local copies, waits for them, and re-layouts  3.13 us
    pallas_call x1, Pallas kernels, given_sums(): pl.pallas_call(given_kernel, out_shape=jax.ShapeDtypeStruct((heads, token...  2.81 us
    pallas_call x1, Pallas kernels, weigh(): pl.pallas_call(kernel, out_shape=(jax.ShapeDtypeStruct((rows, slot_rows),...  2.14 us
    pallas_call x1, Pallas kernels, pack(): pl.pallas_call(lambda *refs: pack_kernel(*refs, per_owner=per_owner), out...  2.13 us
    ppermute x1, starting transfers between devices, per_device(): taken = lax.ppermute(given, 'tensor', neighbours)  1.72 us
  transfers between devices with their start and end apart: 3, of which 1 were waited for; matrix products, arithmetic and copies ran while one was open for 0% of the time, Pallas kernels for 15%

profile of v6, /device:TPU:1, one launch (start us, length us, event | category | flops | bytes accessed | tf_op | source)
XLA Modules:
  0.0 57.2 jit_solution(5764379958602307268)
XLA Ops:
  0.6 2.1 %pack.1 = (bf16[256,1152]{1,0:T(8,128)(2,1)}, s32[64,128]{1,0:T(8,128)}) custom-call(s32[16]{0:T(128)} %refs_0_.3, s32[1024]{0:T(1024)} %refs_1_.2, bf16[4,16,1024]{2,1,0:T(8,128)(2,1)} %refs_6_.1), custom_call_target="tpu_custom_call" | custom-call | tf_op jit(solution)/shard_map/pack/pallas_call | solution.py:84
  2.8 9.6 %all-to-all-start = ((bf16[32,8,1152]{2,1,0:T(8,128)(2,1)}), bf16[32,8,1152]{2,1,0:T(8,128)(2,1)S(1)}, u32[]{:S(2)}, u32[]{:S(2)}) async-start(bf16[32,8,1152]{2,1,0:T(8,128)(2,1)} %bitcast.9), calls=%async_computation | async-start | bytes 1179648 | tf_op jit(solution)/shard_map/all_to_all | solution.py:459
  12.4 0.0 copy-start.1
  12.4 0.0 copy-start.3
  12.4 0.0 copy-start.6
  12.5 2.8 %given.1.refs_2_ = bf16[8,64,128]{2,1,0:T(8,128)(2,1)} custom-call(s32[1]{0:T(128)} %bitcast.2.place.refs_1_, bf16[4,16,1024]{2,1,0:T(8,128)(2,1)} %refs_6_.1, bf16[1024,1024]{1,0:T(8,128)(2,1)} %refs_7_.1, bf16[1024,1024]{1,0:T(8,128)(2,1)} %refs_8_.1), custom_call_target="tpu_custom_call" | custom-call | flops 134217728 | bytes 2097152 | tf_op jit(solution)/shard_map/given/pallas_call | solution.py:137
  15.3 1.7 %collective-permute-start = (bf16[8,64,128]{2,1,0:T(8,128)(2,1)}, bf16[8,64,128]{2,1,0:T(8,128)(2,1)S(1)}, u32[]{:S(2)}, u32[]{:S(2)}) collective-permute-start(bf16[8,64,128]{2,1,0:T(8,128)(2,1)} %given.1.refs_2_), channel_id=1, source_target_pairs={{0,1},{1,0},{2,3},{3,2},{4,5},{5,4},{6,7},{7,6},{8,9},{9,8},{10,11... | collective-permute-start | bytes 393224 | tf_op jit(solution)/shard_map/ppermute | solution.py:470
  17.0 0.0 copy-done.1
  17.0 0.0 copy-done.3
  17.0 0.0 copy-done.6
  17.0 0.0 copy-start.2
  17.0 0.9 %copy-done.2 = bf16[8,64,128]{2,1,0:T(8,128)(2,1)S(1)} copy-done((bf16[8,64,128]{2,1,0:T(8,128)(2,1)S(1)}, bf16[8,64,128]{2,1,0:T(8,128)(2,1)}, u32[]{:S(2)}) %copy-start.2) | copy-done | bytes 131096
  17.9 3.5 %cached.1 = (bf16[8,64,128]{2,1,0:T(8,128)(2,1)S(1)}, f32[512,128]{1,0:T(8,128)S(1)}, f32[512,128]{1,0:T(8,128)S(1)}) custom-call(s32[16]{0:T(128)S(1)} %copy-done.6, s32[1]{0:T(128)} %bitcast.2.place.refs_1_, bf16[8,64,128]{2,1,0:T(8,128)(2,1)S(1)} %copy-done.2, bf16[4,16,1024]{2,1,0:T(8,128)(2,1)S(1)} %copy-done.3, bf16[16,1,256,128]{3,2,1,0:T(8,128)(2,1)} %refs_4_.1, ...), custom_call_target="tpu_custom_call" | custom-call | flops 201326592 | bytes 4194304 | tf_op jit(solution)/shard_map/cached/pallas_call | solution.py:222
  21.4 0.0 collective-permute-done.taken
  21.5 0.0 all-to-all-done
  21.5 0.0 copy-start
  21.5 2.2 %copy-done = bf16[32,64,1024]{2,1,0:T(8,128)(2,1)S(1)} copy-done((bf16[32,64,1024]{2,1,0:T(8,128)(2,1)S(1)}, bf16[32,64,1024]{2,1,0:T(8,128)(2,1)}, u32[]{:S(2)}) %copy-start) | copy-done | bytes 4194328
  23.7 0.0 copy-start.4
  23.7 0.0 copy-start.5
  23.7 1.3 %shrink.1 = (bf16[8,192,128]{2,1,0:T(8,128)(2,1)S(1)}, bf16[256,128]{1,0:T(8,128)(2,1)S(1)}) custom-call(bf16[256,1152]{1,0:T(8,128)(2,1)S(1)} %bitcast.7, bf16[32,64,1024]{2,1,0:T(8,128)(2,1)S(1)} %copy-done, bf16[8,64,128]{2,1,0:T(8,128)(2,1)S(1)} %pair.1.refs_2_), custom_call_target="tpu_custom_call" | custom-call | flops 1073741824 | bytes 4194304 | tf_op jit(solution)/shard_map/shrink/pallas_call | solution.py:278
  25.0 16.7 %all_to_all.27.refs_0_ = bf16[8,192,128]{2,1,0:T(8,128)(2,1)S(1)} all-to-all(bf16[8,192,128]{2,1,0:T(8,128)(2,1)S(1)} %get-tuple-element.21), channel_id=1, replica_groups={{7,6,5,4,3,2,1,0},{15,14,13,12,11,10,9,8},{23,22,21,20,19,18,17,16},{31..., dimensions={0} | all-to-all | bytes 786432 | tf_op jit(solution)/shard_map/all_to_all | solution.py:459
  41.7 0.0 copy-done.4
  41.7 1.2 %expand.1 = (bf16[64,128]{1,0:T(8,128)(2,1)}, bf16[64,128]{1,0:T(8,128)(2,1)S(1)}, f32[64,128]{1,0:T(8,128)S(1)}, bf16[256,128]{1,0:T(8,128)(2,1)}) custom-call(bf16[8,192,128]{2,1,0:T(8,128)(2,1)S(1)} %all_to_all.27.refs_0_, bf16[256,128]{1,0:T(8,128)(2,1)S(1)} %get-tuple-element.22.refs_1_, bf16[32,64,128]{2,1,0:T(8,128)(2,1)S(1)} %copy-done.4), custom_call_target="tpu_custom_call" | custom-call | tf_op jit(solution)/shard_map/expand/pallas_call | solution.py:334
  42.9 9.7 %all-to-all-start.2 = ((bf16[32,8,128]{2,1,0:T(8,128)(2,1)}), bf16[32,8,128]{2,1,0:T(8,128)(2,1)S(1)}, u32[]{:S(2)}, u32[]{:S(2)}) async-start(bf16[32,8,128]{2,1,0:T(8,128)(2,1)} %bitcast.4), calls=%async_computation.2 | async-start | bytes 131072 | tf_op jit(solution)/shard_map/all_to_all | solution.py:459
  52.5 0.0 copy-done.5
  52.5 2.1 %weigh.1 = (bf16[512,256]{1,0:T(8,128)(2,1)S(1)}, f32[512,128]{1,0:T(8,128)S(1)}, bf16[64,256]{1,0:T(8,128)(2,1)S(1)}) custom-call(bf16[4,16,1024]{2,1,0:T(8,128)(2,1)S(1)} %copy-done.3, bf16[64,128]{1,0:T(8,128)(2,1)S(1)} %get-tuple-element.25.refs_1_, f32[64,128]{1,0:T(8,128)S(1)} %get-tuple-element.26.refs_2_.base_values, ...), custom_call_target="tpu_custom_call" | custom-call | flops 16777216 | bytes 1048576 | tf_op jit(solution)/shard_map/weigh/pallas_call | solution.py:391
  54.7 1.6 %all-to-all-done.2 = bf16[32,8,128]{2,1,0:T(8,128)(2,1)S(1)} async-done(((bf16[32,8,128]{2,1,0:T(8,128)(2,1)}), bf16[32,8,128]{2,1,0:T(8,128)(2,1)S(1)}, u32[]{:S(2)}, u32[]{:S(2)}) %all-to-all-start.2) | async-done | bytes 65568 | tf_op jit(solution)/shard_map/all_to_all | solution.py:459
  56.3 0.9 %finish.1 = (bf16[64,128]{1,0:T(8,128)(2,1)}, bf16[4,16,1024]{2,1,0:T(8,128)(2,1)}) custom-call(bf16[256,128]{1,0:T(8,128)(2,1)S(1)} %bitcast.8, bf16[64,256]{1,0:T(8,128)(2,1)S(1)} %get-tuple-element.30.chosen, f32[64,128]{1,0:T(8,128)S(1)} %get-tuple-element.26.refs_2_.base_values, bf16[512,256]{1,0:T(8,128)(2,1)S(1)} %get-tuple-element.31.spread, ...), custom_call_target="tpu_custom_call" | custom-call | tf_op jit(solution)/shard_map/finish/pallas_call | solution.py:428
  (1 shorter events, 0.0 us)
Async XLA Ops:
  2.8 18.7 %all-to-all-start = ((bf16[32,8,1152]{2,1,0:T(8,128)(2,1)}), bf16[32,8,1152]{2,1,0:T(8,128)(2,1)S(1)}, u32[]{:S(2)}, u32[]{:S(2)}) async-start(bf16[32,8,1152]{2,1,0:T(8,128)(2,1)} %bitcast.9), calls=%async_computation | async-start | bytes 1179648 | tf_op jit(solution)/shard_map/all_to_all | solution.py:459
  12.4 4.6 %copy-start.1 = (bf16[4,16,1024]{2,1,0:T(8,128)(2,1)S(1)}, bf16[4,16,1024]{2,1,0:T(8,128)(2,1)}, u32[]{:S(2)}) copy-start(bf16[4,16,1024]{2,1,0:T(8,128)(2,1)} %refs_6_.1) | copy-start | bytes 393220
  12.4 4.6 %copy-start.3 = (bf16[4,16,1024]{2,1,0:T(8,128)(2,1)S(1)}, bf16[4,16,1024]{2,1,0:T(8,128)(2,1)}, u32[]{:S(2)}) copy-start(bf16[4,16,1024]{2,1,0:T(8,128)(2,1)} %refs_0_.5) | copy-start | bytes 393220
  12.4 4.6 %copy-start.6 = (s32[16]{0:T(128)S(1)}, s32[16]{0:T(128)}, u32[]{:S(2)}) copy-start(s32[16]{0:T(128)} %refs_0_.4) | copy-start | bytes 196
  15.3 6.1 %collective-permute-start = (bf16[8,64,128]{2,1,0:T(8,128)(2,1)}, bf16[8,64,128]{2,1,0:T(8,128)(2,1)S(1)}, u32[]{:S(2)}, u32[]{:S(2)}) collective-permute-start(bf16[8,64,128]{2,1,0:T(8,128)(2,1)} %given.1.refs_2_), channel_id=1, source_target_pairs={{0,1},{1,0},{2,3},{3,2},{4,5},{5,4},{6,7},{7,6},{8,9},{9,8},{10,11... | collective-permute-start | bytes 393224 | tf_op jit(solution)/shard_map/ppermute | solution.py:470
  17.0 0.9 %copy-start.2 = (bf16[8,64,128]{2,1,0:T(8,128)(2,1)S(1)}, bf16[8,64,128]{2,1,0:T(8,128)(2,1)}, u32[]{:S(2)}) copy-start(bf16[8,64,128]{2,1,0:T(8,128)(2,1)} %given.1.refs_2_) | copy-start | bytes 393220
  21.5 2.2 %copy-start = (bf16[32,64,1024]{2,1,0:T(8,128)(2,1)S(1)}, bf16[32,64,1024]{2,1,0:T(8,128)(2,1)}, u32[]{:S(2)}) copy-start(bf16[32,64,1024]{2,1,0:T(8,128)(2,1)} %refs_1_.3) | copy-start | bytes 12582916
  23.7 18.0 %copy-start.4 = (bf16[32,64,128]{2,1,0:T(8,128)(2,1)S(1)}, bf16[32,64,128]{2,1,0:T(8,128)(2,1)}, u32[]{:S(2)}) copy-start(bf16[32,64,128]{2,1,0:T(8,128)(2,1)} %refs_2_.3) | copy-start | bytes 1572868
  23.7 28.9 %copy-start.5 = (s32[64,128]{1,0:T(8,128)S(1)}, s32[64,128]{1,0:T(8,128)}, u32[]{:S(2)}) copy-start(s32[64,128]{1,0:T(8,128)} %get-tuple-element.29.refs_5_) | copy-start | bytes 98308
  42.9 13.4 %all-to-all-start.2 = ((bf16[32,8,128]{2,1,0:T(8,128)(2,1)}), bf16[32,8,128]{2,1,0:T(8,128)(2,1)S(1)}, u32[]{:S(2)}, u32[]{:S(2)}) async-start(bf16[32,8,128]{2,1,0:T(8,128)(2,1)} %bitcast.4), calls=%async_computation.2 | async-start | bytes 131072 | tf_op jit(solution)/shard_map/all_to_all | solution.py:459
